TPU v7x, 32 devices: a whole 2x2x4 slice. The times are simulated.
32 devices in a mesh: dp: 2 (over x), tp: 4 (over y, core), fsdp: 4 (over z).
Axes of the slice: x: 2, y: 2, z: 4, core: 2. Of those that a mesh axis runs over, the one named last changes fastest.
Arguments:
- hidden: bfloat16 [8, 2, 128, 2432], P(('dp', 'fsdp')), may hold values from -6 to 6
- text_kv: bfloat16 [8, 2, 333, 24, 128], P(('dp', 'fsdp'), None, None, 'tp'), may hold values from -6 to 6
- mods: bfloat16 [8, 2, 5, 2432], P(('dp', 'fsdp')), may hold values from -5 to 5
- latents: float32 [8, 128, 64], P(('dp', 'fsdp')), may hold values from -6 to 6
- noise: float32 [8, 128, 64], P(('dp', 'fsdp')), may hold values from -6 to 6
- step_index: int32 [8], P(('dp', 'fsdp')), may hold values from 1 to 8
- group_id: int32 [8], P(('dp', 'fsdp')), may hold values from 0 to 3
- advantages: float32 [8], P(('dp', 'fsdp')), may hold values from -4 to 4
- w_qkv: bfloat16 [2432, 3, 1536], P(('dp', 'fsdp'), None, 'tp'), may hold values from -0.125 to 0.125
- w_out: bfloat16 [2432, 1536], P(('dp', 'fsdp'), 'tp'), may hold values from -0.15625 to 0.15625
- w_final: bfloat16 [2432, 64], P(('dp', 'fsdp')), may hold values from -0.125 to 0.125
Outputs:
- next_latents: float32 [8, 128, 64], P(('dp', 'fsdp'))
- log_prob: float32 [8], P(('dp', 'fsdp'))
- grad_out: float32 [2432, 1536], P(('dp', 'fsdp'), 'tp')
- grad_final: float32 [2432, 64], P(('dp', 'fsdp'))
All inputs are finite; a program needn't handle non-finite values.
Results may differ from a plain program's by a relative error of at most 0.006.
Values may be sent and summed in bfloat16 or wider, within the bound.
A program may use at most 64 MiB of HBM per device.

v0:
```python
import math

import jax
import jax.numpy as jnp
from jax import lax
from jax.sharding import PartitionSpec as P

STEPS = 10
GROUPS = 4


eps_norm = 1e-06
time_shift = 3.0
noise_level = 0.7
guidance = 4.5
loss_scale = 2048.0


def layer_norm(values):
    centred = values - jnp.mean(values, axis=-1, keepdims=True)
    inverse = lax.rsqrt(jnp.mean(centred * centred, axis=-1, keepdims=True) + eps_norm)
    return (centred * inverse, inverse)


def layer_norm_back(upstream, normed, inverse):
    return inverse * (
        upstream
        - jnp.mean(upstream, axis=-1, keepdims=True)
        - normed * jnp.mean(upstream * normed, axis=-1, keepdims=True)
    )


def rms_norm(values):
    inverse = lax.rsqrt(jnp.mean(values * values, axis=-1, keepdims=True) + eps_norm)
    return values * inverse


def plan(sample_step, step_count):
    level_now = 1.0 - sample_step.astype(jnp.float32) / step_count
    level_next = 1.0 - (sample_step + 1).astype(jnp.float32) / step_count
    time_now = time_shift * level_now / (1.0 + (time_shift - 1.0) * level_now)
    time_next = time_shift * level_next / (1.0 + (time_shift - 1.0) * level_next)
    noise_scale = noise_level * jnp.sqrt(time_now / (1.0 - time_now))
    return (time_now, time_now - time_next, noise_scale)


def transition(latent, noise_draw, velocity, sample_step, step_count):
    time_now, step_size, noise_scale = plan(sample_step, step_count)
    spread = noise_scale * jnp.sqrt(step_size)
    drift_velocity = 1.0 + noise_scale * noise_scale * (1.0 - time_now) / (2.0 * time_now)
    drift_latent = noise_scale * noise_scale / (2.0 * time_now)
    centre = latent - step_size * (drift_velocity * velocity + drift_latent * latent)
    following = centre + spread * noise_draw
    offset = following - centre
    log_density = jnp.mean(
        -offset * offset / (2.0 * spread * spread) - jnp.log(spread) - 0.5 * math.log(2.0 * math.pi)
    )
    slope = step_size * drift_velocity * offset / (spread * spread * offset.size)
    return (following, log_density, slope)


def attend(projected, text_pair):
    head_width = projected.shape[-1]
    query = rms_norm(projected[:, :, 0])
    key_image = rms_norm(projected[:, :, 1])
    key_text = rms_norm(text_pair[..., :head_width].astype(jnp.float32))
    query_half = query.astype(jnp.bfloat16)
    key_all = jnp.concatenate([key_image.astype(jnp.bfloat16), key_text.astype(jnp.bfloat16)], 1)
    value_all = jnp.concatenate(
        [projected[:, :, 2].astype(jnp.bfloat16), text_pair[..., head_width:]], 1
    )
    score_scale = 1.0 / math.sqrt(head_width)
    scores = (
        jnp.einsum("bqhe,bkhe->bhqk", query_half, key_all, preferred_element_type=jnp.float32)
        * score_scale
    )
    exponent = jnp.exp(scores)
    attention = exponent / jnp.sum(exponent, axis=-1, keepdims=True)
    attention_half = attention.astype(jnp.bfloat16)
    return jnp.einsum(
        "bhqk,bkhe->bqhe", attention_half, value_all, preferred_element_type=jnp.float32
    ).astype(jnp.bfloat16)


def project(attended_rows, out_rows):
    last = attended_rows.ndim - 1
    return lax.dot_general(
        attended_rows, out_rows, (((last,), (1,)), ((), ())), preferred_element_type=jnp.float32
    )


def head_total(partial_sum):
    return lax.psum(partial_sum, "tp")


def contract_rows(left, right):
    return lax.dot_general(
        left, right, (((0,), (0,)), ((), ())), preferred_element_type=jnp.float32
    )


def local(
    hidden, text_kv, mods, latents, noise, step_index, group_id, advantages, w_qkv, w_out, w_final
):
    row_count = hidden.shape[2]
    model_width = hidden.shape[3]
    heads = text_kv.shape[3]
    head_width = text_kv.shape[4] // 2
    head_columns = heads * head_width
    local_columns = 3 * head_columns
    residual = hidden[0].astype(jnp.float32)
    mod_values = mods[0].astype(jnp.float32)
    normed, inverse = layer_norm(residual)
    modulated = (normed * (1.0 + mod_values[:, 1:2]) + mod_values[:, 0:1]).astype(jnp.bfloat16)
    stacked = modulated.reshape(2 * row_count, model_width)
    piece = lax.all_gather(w_qkv, ("dp", "fsdp"), axis=0, tiled=True)
    projected = jnp.dot(
        stacked, piece.reshape(piece.shape[0], local_columns), preferred_element_type=jnp.float32
    )
    out_rows, final_rows = (
        lax.all_gather(w_out, ("dp", "fsdp"), axis=0, tiled=True),
        lax.all_gather(w_final, ("dp", "fsdp"), axis=0, tiled=True),
    )
    projected = projected.reshape(2, row_count, 3, heads, head_width)
    attended = attend(projected, text_kv[0])
    attended_flat = attended.reshape(2, row_count, head_columns)
    partial_sum = jnp.stack(
        [head_total(project(attended_flat[which], out_rows)) for which in range(2)], 0
    )
    updated = residual + mod_values[:, 2:3] * partial_sum
    final_normed, final_inverse = layer_norm(updated)
    readout = (final_normed * (1.0 + mod_values[:, 4:5]) + mod_values[:, 3:4]).astype(jnp.bfloat16)
    velocity = jnp.einsum("brd,dp->brp", readout, final_rows, preferred_element_type=jnp.float32)
    guided = velocity[1] + guidance * (velocity[0] - velocity[1])
    following, log_density, slope = transition(latents[0], noise[0], guided, step_index[0], STEPS)
    onehot = (group_id[0] == jnp.arange(GROUPS, dtype=jnp.int32)).astype(jnp.float32)
    counts = lax.psum(onehot, ("dp", "fsdp"))
    members = jnp.sum(onehot * counts)
    sample_weight = loss_scale * advantages[0] / members
    upstream_velocity = sample_weight * slope
    velocity_grad = jnp.stack(
        [guidance * upstream_velocity, (1.0 - guidance) * upstream_velocity], 0
    ).astype(jnp.bfloat16)
    readout_grad = jnp.einsum(
        "brp,dp->brd", velocity_grad, final_rows, preferred_element_type=jnp.float32
    )
    updated_grad = layer_norm_back(
        readout_grad * (1.0 + mod_values[:, 4:5]), final_normed, final_inverse
    )
    partial_grad = (mod_values[:, 2:3] * updated_grad).astype(jnp.bfloat16)
    readout_flat = readout.reshape(2 * row_count, model_width)
    velocity_flat = velocity_grad.reshape(2 * row_count, -1)
    partial_flat = partial_grad.reshape(2 * row_count, model_width)
    attended_rows = attended_flat.reshape(2 * row_count, head_columns)
    grad_out, grad_final = (
        lax.psum_scatter(
            contract_rows(partial_flat, attended_rows),
            ("dp", "fsdp"),
            scatter_dimension=0,
            tiled=True,
        ),
        lax.psum_scatter(
            contract_rows(readout_flat, velocity_flat),
            ("dp", "fsdp"),
            scatter_dimension=0,
            tiled=True,
        ),
    )
    return (following[None], log_density[None], grad_out, grad_final)


def solution(mesh):
    in_specs = (
        P(("dp", "fsdp"), None, None, None),
        P(("dp", "fsdp"), None, None, "tp", None),
        P(("dp", "fsdp"), None, None, None),
        P(("dp", "fsdp"), None, None),
        P(("dp", "fsdp"), None, None),
        P(("dp", "fsdp")),
        P(("dp", "fsdp")),
        P(("dp", "fsdp")),
        P(("dp", "fsdp"), None, "tp"),
        P(("dp", "fsdp"), "tp"),
        P(("dp", "fsdp"), None),
    )
    out_specs = (
        P(("dp", "fsdp"), None, None),
        P(("dp", "fsdp")),
        P(("dp", "fsdp"), "tp"),
        P(("dp", "fsdp"), None),
    )
    return jax.shard_map(local, mesh=mesh, in_specs=in_specs, out_specs=out_specs, check_vma=False)
```

profile of v0, /device:TPU:0, one launch (start us, length us, event | category | flops | bytes accessed | tf_op | source)
XLA Modules:
  0.0 378.3 jit_solution(213395365241709139)
XLA Ops:
  7.2 0.7 all-gather.4.cloned.1.call-update
  8.0 0.7 all-gather.6.cloned.1.call-update
  8.7 1.5 convert_reduce_fusion
  10.3 0.5 fusion.4
  10.8 1.9 copy.22
  13.0 0.9 slice.66
  14.0 89.7 %all-gather.4.cloned.1.call-done = bf16[2432,3,384]{2,0,1:T(8,128)(2,1)} async-done(((bf16[304,3,384]{2,0,1:T(8,128)(2,1)}), bf16[2432,3,384]{2,0,1:T(8,128)(2,1)}) %all-gather.4.cloned.1.call-update) | async-done | bytes 5603344 | tf_op jit(solution)/shard_map/all_gather | solution.py:116
  103.6 8.7 %copy.21 = bf16[2432,3,384]{0,2,1:T(8,128)(2,1)} copy(bf16[2432,3,384]{2,0,1:T(8,128)(2,1)} %all-gather.4.cloned.1.call-done) | data formatting | bytes 11206656 | tf_op jit(solution)/shard_map/all_gather | solution.py:116
  112.4 4.0 %fusion.11 = f32[2,128,3,6,64]{1,4,3,2,0:T(8,128)S(1)} fusion(bf16[3,6,64,2432,1]{3,2,1,0,4:T(8,128)(2,1)} %bitcast.132, bf16[1,2,128,2432]{3,2,1,0:T(8,128)(2,1)S(1)} %copy-done, f32[2,2432]{1,0:T(2,128)S(1)} %get-tuple-element.19, f32[2,2432]{1,0:T(2,128)S(1)} %get-tuple-element.20, f32[2,128]{1,0:T(2,128)S(1)} %add_rsqrt_fusion.4, ...), kind=kOutput, calls=%fused_computation.28 | convolution fusion | flops 1438187520 | bytes 8069120 | tf_op jit(solution)/shard_map/dot_general | solution.py:117
  116.6 0.8 fusion.2
  117.6 0.6 fusion.20
  118.3 32.3 %all-gather.6.cloned.1.call-done = bf16[2432,384]{1,0:T(8,128)(2,1)} async-done(((bf16[304,384]{1,0:T(8,128)(2,1)}), bf16[2432,384]{1,0:T(8,128)(2,1)}) %all-gather.6.cloned.1.call-update) | async-done | bytes 1867792 | tf_op jit(solution)/shard_map/all_gather | solution.py:121
  150.5 3.4 convolution_bitcast_fusion.1
  153.9 1.8 convolution_bitcast_fusion.2
  156.4 19.6 %psum.23 = f32[4]{0:T(128)S(1)} all-reduce(f32[4]{0:T(128)S(1)} %compare_convert_fusion), channel_id=1, replica_groups=mesh['dp'=2,'tp'=4,'fsdp'=4] {'dp','fsdp'}, use_global_device_ids=true, to_apply=%region_11.0 | all-reduce | flops 4 | bytes 32 | tf_op jit(solution)/shard_map/psum | solution.py:137
  177.7 31.9 %all-gather = bf16[8,304,64]{1,2,0:T(8,128)(2,1)S(1)} all-gather(bf16[1,304,64]{1,2,0:T(8,128)(2,1)S(1)} %bitcast.136), channel_id=1, replica_groups=mesh['dp'=2,'tp'=4,'fsdp'=4] {'dp','fsdp'}, dimensions={0}, use_global_device_ids=true | all-gather | bytes 350208 | tf_op jit(solution)/shard_map/all_gather | solution.py:122
  209.6 0.2 copy.23
  209.8 0.3 reshape.152
  210.1 0.6 fusion.46
  211.4 0.2 copy.24
  211.6 1.3 all-reduce.3.cloned.1.call-done
  212.9 2.4 fusion.53
  215.4 0.4 multiply_reduce_fusion.1
  215.8 0.6 fusion.45
  216.5 1.9 convolution_bitcast_fusion
  218.4 2.2 fusion.52
  220.7 2.9 multiply_convert_fusion
  223.5 2.7 fusion.29
  226.3 0.6 fusion.42
  227.5 57.5 %reduce-scatter.7.cloned.1.call-done = f32[304,64]{1,0:T(8,128)} async-done(((f32[2432,64]{1,0:T(8,128)}), f32[304,64]{1,0:T(8,128)}) %reduce-scatter.7.cloned.1.call-update) | async-done | bytes 77840
  285.0 1.7 copy.27
  286.7 84.0 %reduce-scatter.5.cloned.1.call-done = f32[304,384]{1,0:T(8,128)} async-done(((f32[2432,384]{1,0:T(8,128)}), f32[304,384]{1,0:T(8,128)}) %reduce-scatter.5.cloned.1.call-update) | async-done | bytes 466960 | tf_op jit(solution)/shard_map/reduce_scatter | solution.py:156
  (45 shorter events, 1.1 us)
Async XLA Ops:
  7.2 3.1 copy-start
  7.2 3.6 copy-start.8
  7.2 3.6 copy-start.2
  7.2 96.4 %all-gather.4.cloned.1.call-start = ((), (), s32[]{:S(2)}) async-start(), calls=%async_computation.2 | async-start | bytes 6303744 | tf_op jit(solution)/shard_map/all_gather | solution.py:116
  7.9 142.6 %all-gather.6.cloned.1.call-start = ((), (), s32[]{:S(2)}) async-start(), calls=%async_computation.3 | async-start | bytes 2101248 | tf_op jit(solution)/shard_map/all_gather | solution.py:121
  8.7 204.2 %all-reduce.3.cloned.1.call-start = ((), (), s32[]{:S(2)}) async-start(), calls=%async_computation.6 | async-start | bytes 4980736 | tf_op jit(solution)/shard_map/psum | solution.py:93
  116.5 1.1 copy-start.3
  150.5 3.4 copy-start.1
  153.9 23.7 %copy-start.7 = (bf16[304,64]{0,1:T(8,128)(2,1)S(1)}, bf16[304,64]{0,1:T(8,128)(2,1)}, u32[]{:S(2)}) copy-start(bf16[304,64]{0,1:T(8,128)(2,1)} %param.21) | copy-start | bytes 116740
  155.7 129.3 %reduce-scatter.7.cloned.1.call-start = ((), (), s32[]{:S(2)}) async-start(), calls=%async_computation.5 | async-start | bytes 1400832
  215.3 1.1 copy-start.4
  215.4 1.1 copy-start.5
  216.5 4.1 %copy-start.6 = (f32[1,128,64]{1,2,0:T(8,128)}, f32[1,128,64]{1,2,0:T(8,128)S(1)}, u32[]{:S(2)}) copy-start(f32[1,128,64]{1,2,0:T(8,128)S(1)} %get-tuple-element.11) | copy-start | bytes 98308
  220.6 150.1 %reduce-scatter.5.cloned.1.call-start = ((), (), s32[]{:S(2)}) async-start(), calls=%async_computation.4 | async-start | bytes 4202496 | tf_op jit(solution)/shard_map/reduce_scatter | solution.py:156
Sparse Core Ops, SparseCore 0:
  10.3 93.3 all-gather.3
  105.7 44.7 all-gather.5
  155.8 57.0 all-reduce.2
  220.7 64.2 reduce-scatter.6
  289.1 81.5 reduce-scatter.4
where the time goes:
time: 379 us; the launch traced here: 378 us
  waiting for transfers between devices  266 us (70%)
  blocking collectives  51.5 us (14%)
  between operations  18.8 us (5%)
  matrix products  17.9 us (5%)
  local copies, waits for them, and re-layouts  14.2 us (4%)
  other arithmetic  9.5 us (3%)
    all_gather x1, waiting for transfers between devices, local(): piece = lax.all_gather(w_qkv, ('dp', 'fsdp'), axis=0, tiled=True)  89.7 us
    reduce_scatter x1, waiting for transfers between devices, local(): lax.psum_scatter(contract_rows(partial_flat, attended_rows), ('dp', 'fsdp...  84 us
    unnamed x6, waiting for transfers between devices  58.9 us
    all_gather x1, waiting for transfers between devices, local(): lax.all_gather(w_out, ('dp', 'fsdp'), axis=0, tiled=True)  32.3 us
    all_gather x1, blocking collectives, local(): lax.all_gather(w_final, ('dp', 'fsdp'), axis=0, tiled=True)  31.9 us
    psum x1, blocking collectives, local(): counts = lax.psum(onehot, ('dp', 'fsdp'))  19.6 us
    all_gather x1, local copies, waits for them, and re-layouts, local(): piece = lax.all_gather(w_qkv, ('dp', 'fsdp'), axis=0, tiled=True)  8.72 us
  transfers between devices with their start and end apart: 5, of which 5 were waited for; matrix products, arithmetic and copies ran while one was open for 8% of the time, Pallas kernels for 0%

commit v1 on v0

--- a/solution.py
+++ b/solution.py
@@ -1,12 +1,16 @@
+import functools
 import math
 
 import jax
 import jax.numpy as jnp
 from jax import lax
+from jax.experimental import pallas as pl
+from jax.experimental.pallas import tpu as pltpu
 from jax.sharding import PartitionSpec as P
 
 STEPS = 10
 GROUPS = 4
+ROW_FIRST = (3, 4)
 
 
 eps_norm = 1e-06
@@ -82,15 +86,323 @@
     ).astype(jnp.bfloat16)
 
 
-def project(attended_rows, out_rows):
-    last = attended_rows.ndim - 1
-    return lax.dot_general(
-        attended_rows, out_rows, (((last,), (1,)), ((), ())), preferred_element_type=jnp.float32
-    )
-
-
-def head_total(partial_sum):
-    return lax.psum(partial_sum, "tp")
+def greet(peers):
+    barrier = pltpu.get_barrier_semaphore()
+    for there, peer in peers:
+        @pl.when(there)
+        def _():
+            pl.semaphore_signal(
+                barrier, inc=1, device_id=peer, device_id_type=pl.DeviceIdType.MESH
+            )
+    pl.semaphore_wait(barrier, sum(jnp.where(there, 1, 0) for there, _ in peers))
+
+
+def remote(src, dst, send_sem, recv_sem, peer):
+    return pltpu.make_async_remote_copy(
+        src_ref=src,
+        dst_ref=dst,
+        send_sem=send_sem,
+        recv_sem=recv_sem,
+        device_id=peer,
+        device_id_type=pl.DeviceIdType.MESH,
+    )
+
+
+def around(dp_size, line_size):
+    row, spot = lax.axis_index("dp"), lax.axis_index("fsdp")
+    across = [{"dp": lax.rem(row + k, dp_size)} for k in range(1, dp_size)]
+    right, left = {"fsdp": lax.rem(spot + 1, line_size)}, {
+        "fsdp": lax.rem(spot + line_size - 1, line_size)
+    }
+    has_right, has_left = spot < line_size - 1, spot > 0
+    peers = [(row >= 0, peer) for peer in across] + [(has_right, right), (has_left, left)]
+    return row, spot, across, (right, left), (has_right, has_left), peers
+
+
+def gather_kernel(
+    dp_size, line_size, row_first, blocks_ref, thin_ref, all_ref, all_thin_ref,
+    local_sem, recv_sem, line_sem, across_sem,
+):
+    row, spot, across, sides, has_side, peers = around(dp_size, line_size)
+    count = blocks_ref.shape[0]
+    me = row * line_size + spot
+
+    def mine(k):
+        return blocks_ref.at[k] if k < count else thin_ref
+
+    def slot(k, which):
+        return all_ref.at[k, which] if k < count else all_thin_ref.at[which]
+
+    def along(k, which, side, own):
+        src = mine(k) if own else slot(k, which)
+        return remote(
+            src, slot(k, which), line_sem.at[side, k, which], recv_sem.at[k, which], sides[side]
+        )
+
+    def over(k, stop, hop, own):
+        which = row * line_size + stop
+        src = mine(k) if own else slot(k, which)
+        return remote(
+            src, slot(k, which), across_sem.at[hop, k, stop], recv_sem.at[k, which], across[hop]
+        )
+
+    def arrived(k, which):
+        along(k, which, 0, False).wait_recv()
+
+    def when(condition, action):
+        @pl.when(condition)
+        def _():
+            action()
+
+    order = list(range(count + 1))
+    greet(peers)
+    keep = [pltpu.make_async_copy(mine(k), slot(k, me), local_sem.at[k]) for k in order]
+    started = []
+
+    def go(condition, copy):
+        when(condition, lambda: copy.start())
+        started.append((condition, copy))
+
+    always = row >= 0
+
+    def own_sends(k):
+        for side in (0, 1):
+            go(has_side[side], along(k, me, side, True))
+        for hop in range(dp_size - 1):
+            go(always, over(k, spot, hop, True))
+
+    first = [k for k in order if k in row_first]
+    rest = [k for k in order if k not in row_first]
+    for k in rest:
+        own_sends(k)
+    for copy in keep:
+        copy.start()
+
+    def pass_on(k, step, hop):
+        from_row = row if hop is None else lax.rem(row + dp_size - hop - 1, dp_size)
+        for side in (0, 1):
+            stop = spot - step if side == 0 else spot + step
+            there = stop >= 0 if side == 0 else stop < line_size
+            safe = lax.rem(stop + line_size, line_size)
+            which = from_row * line_size + safe
+            when(there, functools.partial(arrived, k, which))
+            go(there & has_side[side], along(k, which, side, False))
+            if k not in row_first:
+                for other in range(dp_size - 1):
+                    go(there, over(k, safe, other, False))
+
+    def row_arrivals(k):
+        for hop in range(dp_size - 1):
+            which = lax.rem(row + dp_size - hop - 1, dp_size) * line_size + spot
+            arrived(k, which)
+            if k in row_first:
+                for side in (0, 1):
+                    go(has_side[side], along(k, which, side, False))
+
+    for step in range(1, line_size):
+        for k in rest:
+            pass_on(k, step, None)
+        if step == 1:
+            for k in first:
+                own_sends(k)
+    for k in first:
+        row_arrivals(k)
+    for step in range(1, line_size):
+        for k in first:
+            for hop in [None] + list(range(dp_size - 1)):
+                pass_on(k, step, hop)
+    for k in rest:
+        for stop in range(line_size):
+            for hop in range(dp_size - 1):
+                arrived(k, lax.rem(row + dp_size - hop - 1, dp_size) * line_size + stop)
+    for copy in keep:
+        copy.wait()
+    for condition, copy in started:
+        when(condition, functools.partial(copy.wait_send))
+
+
+def gather_rows(blocks, thin, dp_size, line_size):
+    kinds = blocks.shape[0] + 1
+    total = dp_size * line_size
+    dma = pltpu.SemaphoreType.DMA
+    return pl.pallas_call(
+        functools.partial(gather_kernel, dp_size, line_size, ROW_FIRST),
+        out_shape=(
+            jax.ShapeDtypeStruct((blocks.shape[0], total) + blocks.shape[1:], blocks.dtype),
+            jax.ShapeDtypeStruct((total,) + thin.shape, thin.dtype),
+        ),
+        in_specs=[pl.BlockSpec(memory_space=pl.ANY)] * 2,
+        out_specs=(pl.BlockSpec(memory_space=pl.ANY),) * 2,
+        scratch_shapes=[
+            dma((kinds,)),
+            dma((kinds, total)),
+            dma((2, kinds, total)),
+            dma((max(dp_size - 1, 1), kinds, line_size)),
+        ],
+        compiler_params=pltpu.CompilerParams(collective_id=0, has_side_effects=True),
+    )(blocks, thin)
+
+
+def scatter_kernel(
+    dp_size, line_size, part_ref, out_ref, row_in, line_in, line_out,
+    row_send, row_recv, line_send, line_recv,
+):
+    row, spot, across, sides, has_side, peers = around(dp_size, line_size)
+
+    def over(stop, hop):
+        target = lax.rem(row + hop + 1, dp_size) * line_size + stop
+        return remote(
+            part_ref.at[target], row_in.at[hop, stop], row_send.at[hop, stop],
+            row_recv.at[hop, stop], across[hop],
+        )
+
+    def along(stop, side):
+        return remote(
+            line_out.at[stop], line_in.at[side, stop], line_send.at[stop],
+            line_recv.at[side, stop], sides[side],
+        )
+
+    def row_sum(stop):
+        value = part_ref[row * line_size + stop].astype(jnp.float32)
+        for hop in range(dp_size - 1):
+            over(stop, hop).wait_recv()
+            value = value + row_in[hop, stop].astype(jnp.float32)
+        return value
+
+    def launch(stop):
+        for hop in range(dp_size - 1):
+            over(stop, hop).start()
+
+    def step(stop, side):
+        from_side = has_side[1 - side]
+        line_out[stop] = row_sum(stop).astype(line_out.dtype)
+
+        @pl.when(from_side)
+        def _():
+            along(stop, side).wait_recv()
+            line_out[stop] = (
+                line_out[stop].astype(jnp.float32) + line_in[side, stop].astype(jnp.float32)
+            ).astype(line_out.dtype)
+
+        along(stop, side).start()
+
+    greet(peers)
+    turns = []
+    for turn in range(line_size - 1):
+        turns.append((line_size - 1 - turn, 0))
+        turns.append((turn, 1))
+    for stop, side in turns:
+        @pl.when(stop > spot if side == 0 else stop < spot)
+        def _():
+            launch(stop)
+    launch(spot)
+    for stop, side in turns:
+        @pl.when(stop > spot if side == 0 else stop < spot)
+        def _():
+            step(stop, side)
+    out_ref[...] = row_sum(spot)
+    for side in (0, 1):
+        @pl.when(has_side[1 - side])
+        def _():
+            along(spot, side).wait_recv()
+            out_ref[...] = out_ref[...] + line_in[side, spot].astype(jnp.float32)
+    for stop in range(line_size):
+        for hop in range(dp_size - 1):
+            over(stop, hop).wait_send()
+    for stop, side in turns:
+        @pl.when(stop > spot if side == 0 else stop < spot)
+        def _():
+            along(stop, side).wait_send()
+
+
+def scatter_rows(parts, dp_size, line_size):
+    block = parts.shape[1:]
+    hops = max(dp_size - 1, 1)
+    dma = pltpu.SemaphoreType.DMA
+    return pl.pallas_call(
+        functools.partial(scatter_kernel, dp_size, line_size),
+        out_shape=jax.ShapeDtypeStruct(block, jnp.float32),
+        in_specs=[pl.BlockSpec(memory_space=pltpu.VMEM)],
+        out_specs=pl.BlockSpec(memory_space=pltpu.VMEM),
+        scratch_shapes=[
+            pltpu.VMEM((hops, line_size) + block, jnp.bfloat16),
+            pltpu.VMEM((2, line_size) + block, jnp.bfloat16),
+            pltpu.VMEM((line_size,) + block, jnp.bfloat16),
+            dma((hops, line_size)),
+            dma((hops, line_size)),
+            dma((line_size,)),
+            dma((2, line_size)),
+        ],
+        compiler_params=pltpu.CompilerParams(
+            collective_id=1, has_side_effects=True, vmem_limit_bytes=48 * 1024 * 1024
+        ),
+    )(parts)
+
+
+def heads_kernel(
+    attended_ref, rows_ref, out_ref, total, out_first, in_first, out_second, in_second,
+    send_sem, recv_sem,
+):
+    me = lax.axis_index("tp")
+    low, high = lax.rem(me, 2), me // 2
+    near, far = {"tp": me + 1 - 2 * low}, {"tp": lax.rem(me + 2, 4)}
+    greet([(me >= 0, near), (me >= 0, far)])
+
+    def product(which):
+        return lax.dot_general(
+            attended_ref[which], rows_ref[...], (((1,), (1,)), ((), ())),
+            preferred_element_type=jnp.float32,
+        )
+
+    half = total.shape[1]
+    out_first[...] = product(1 - low).astype(jnp.bfloat16)
+    first = remote(out_first, in_first, send_sem.at[0], recv_sem.at[0], near)
+    first.start()
+    total[...] = product(low).reshape(total.shape)
+    first.wait_recv()
+    total[...] = total[...] + in_first[...].reshape(total.shape).astype(jnp.float32)
+    out_second[...] = total[1 - high].astype(jnp.bfloat16)
+    second = remote(out_second, in_second, send_sem.at[1], recv_sem.at[1], far)
+    second.start()
+    second.wait_recv()
+    out_ref[low, high] = (total[high] + in_second[...].astype(jnp.float32)).astype(jnp.bfloat16)
+    done = out_ref.at[low, high]
+    third = remote(done, done, send_sem.at[2], recv_sem.at[2], far)
+    third.start()
+    fourth = remote(done, done, send_sem.at[3], recv_sem.at[3], near)
+    fourth.start()
+    remote(done, out_ref.at[low, 1 - high], send_sem.at[2], recv_sem.at[2], far).wait_recv()
+    other = out_ref.at[low, 1 - high]
+    fifth = remote(other, other, send_sem.at[4], recv_sem.at[4], near)
+    fifth.start()
+    fourth.wait_recv()
+    fifth.wait_recv()
+    for copy in (first, second, third, fourth, fifth):
+        copy.wait_send()
+
+
+def head_sum(attended, out_rows):
+    _, tokens, _ = attended.shape
+    width = out_rows.shape[0]
+    half = tokens // 2
+    return pl.pallas_call(
+        heads_kernel,
+        out_shape=jax.ShapeDtypeStruct((2, 2, half, width), jnp.bfloat16),
+        in_specs=[pl.BlockSpec(memory_space=pltpu.VMEM)] * 2,
+        out_specs=pl.BlockSpec(memory_space=pltpu.VMEM),
+        scratch_shapes=[
+            pltpu.VMEM((2, half, width), jnp.float32),
+            pltpu.VMEM((tokens, width), jnp.bfloat16),
+            pltpu.VMEM((tokens, width), jnp.bfloat16),
+            pltpu.VMEM((half, width), jnp.bfloat16),
+            pltpu.VMEM((half, width), jnp.bfloat16),
+            pltpu.SemaphoreType.DMA((5,)),
+            pltpu.SemaphoreType.DMA((5,)),
+        ],
+        compiler_params=pltpu.CompilerParams(
+            collective_id=2, has_side_effects=True, vmem_limit_bytes=48 * 1024 * 1024
+        ),
+    )(attended, out_rows).reshape(2, tokens, width)
 
 
 def contract_rows(left, right):
@@ -107,26 +419,24 @@
     heads = text_kv.shape[3]
     head_width = text_kv.shape[4] // 2
     head_columns = heads * head_width
-    local_columns = 3 * head_columns
     residual = hidden[0].astype(jnp.float32)
     mod_values = mods[0].astype(jnp.float32)
     normed, inverse = layer_norm(residual)
     modulated = (normed * (1.0 + mod_values[:, 1:2]) + mod_values[:, 0:1]).astype(jnp.bfloat16)
     stacked = modulated.reshape(2 * row_count, model_width)
-    piece = lax.all_gather(w_qkv, ("dp", "fsdp"), axis=0, tiled=True)
-    projected = jnp.dot(
-        stacked, piece.reshape(piece.shape[0], local_columns), preferred_element_type=jnp.float32
-    )
-    out_rows, final_rows = (
-        lax.all_gather(w_out, ("dp", "fsdp"), axis=0, tiled=True),
-        lax.all_gather(w_final, ("dp", "fsdp"), axis=0, tiled=True),
+    dp_size, line_size = lax.axis_size("dp"), lax.axis_size("fsdp")
+    blocks = jnp.concatenate([jnp.swapaxes(w_qkv, 0, 1), w_out[None]], 0)
+    gathered, final_rows = gather_rows(blocks, w_final, dp_size, line_size)
+    gathered = gathered.reshape(4, model_width, head_columns)
+    final_rows = final_rows.reshape(model_width, -1)
+    out_rows = gathered[3]
+    projected = jnp.stack(
+        [jnp.dot(stacked, gathered[k], preferred_element_type=jnp.float32) for k in range(3)], 1
     )
     projected = projected.reshape(2, row_count, 3, heads, head_width)
     attended = attend(projected, text_kv[0])
     attended_flat = attended.reshape(2, row_count, head_columns)
-    partial_sum = jnp.stack(
-        [head_total(project(attended_flat[which], out_rows)) for which in range(2)], 0
-    )
+    partial_sum = head_sum(attended_flat, out_rows).astype(jnp.float32)
     updated = residual + mod_values[:, 2:3] * partial_sum
     final_normed, final_inverse = layer_norm(updated)
     readout = (final_normed * (1.0 + mod_values[:, 4:5]) + mod_values[:, 3:4]).astype(jnp.bfloat16)
@@ -152,20 +462,17 @@
     velocity_flat = velocity_grad.reshape(2 * row_count, -1)
     partial_flat = partial_grad.reshape(2 * row_count, model_width)
     attended_rows = attended_flat.reshape(2 * row_count, head_columns)
-    grad_out, grad_final = (
-        lax.psum_scatter(
-            contract_rows(partial_flat, attended_rows),
-            ("dp", "fsdp"),
-            scatter_dimension=0,
-            tiled=True,
-        ),
-        lax.psum_scatter(
-            contract_rows(readout_flat, velocity_flat),
-            ("dp", "fsdp"),
-            scatter_dimension=0,
-            tiled=True,
-        ),
-    )
+    parts = jnp.concatenate(
+        [
+            contract_rows(partial_flat, attended_rows).astype(jnp.bfloat16),
+            contract_rows(readout_flat, velocity_flat).astype(jnp.bfloat16),
+        ],
+        1,
+    )
+    sums = scatter_rows(
+        parts.reshape(dp_size * line_size, -1, parts.shape[1]), dp_size, line_size
+    )
+    grad_out, grad_final = sums[:, :head_columns], sums[:, head_columns:]
     return (following[None], log_density[None], grad_out, grad_final)
 
 

time: 379 us -> 237 us (0.63)
  waiting for transfers between devices: 266 us -> 0 us
  Pallas kernels: 0 us -> 151 us
  blocking collectives: 51.5 us -> 20.8 us
  local copies, waits for them, and re-layouts: 14.2 us -> 29.6 us
  between operations: 18.8 us -> 5.7 us
  other arithmetic: 9.5 us -> 13.7 us
    pallas_call x0 -> x3, Pallas kernels: none -> 151 us  [the longest x1 91.8 us: gather_rows(): pl.pallas_call(functools.partial(gather_kernel, dp_size, line_size, ROW_F...]
    all_gather x2 -> x0, waiting for transfers between devices: 122 us -> none  [the longest x1 89.7 us: local(): piece = lax.all_gather(w_qkv, ('dp', 'fsdp'), axis=0, tiled=True)]
    reduce_scatter x1 -> x0, waiting for transfers between devices: 84 us -> none  [local(): lax.psum_scatter(contract_rows(partial_flat, attended_rows), ('dp', 'fsdp...]
    unnamed x6 -> x0, waiting for transfers between devices: 58.9 us -> none
    all_gather x1 -> x0, blocking collectives: 31.9 us -> none  [local(): lax.all_gather(w_final, ('dp', 'fsdp'), axis=0, tiled=True)]
    all_gather x2 -> x0, local copies, waits for them, and re-layouts: 8.95 us -> none  [the longest x1 8.72 us: local(): piece = lax.all_gather(w_qkv, ('dp', 'fsdp'), axis=0, tiled=True)]
    dot_general x0 -> x2, local copies, waits for them, and re-layouts: none -> 7.99 us  [local(): jnp.dot(stacked, gathered[k], preferred_element_type=jnp.float32)]
    slice x1 -> x3, local copies, waits for them, and re-layouts: 0.02 us -> 6.64 us  [the longest x1 5.8 us: local(): out_rows = gathered[3]]
  transfers between devices with their start and end apart: 5 -> 0, of which waited for: 5 -> 0; matrix products, arithmetic and copies ran while one was open for 8% -> 0% of each run, Pallas kernels for 0% -> 0%
where the time goes in v1:
time: 237 us; the launch traced here: 236 us
  Pallas kernels  151 us (64%)
  local copies, waits for them, and re-layouts  29.6 us (12%)
  blocking collectives  20.8 us (9%)
  matrix products  15 us (6%)
  other arithmetic  13.7 us (6%)
  between operations  5.7 us (2%)
    pallas_call x1, Pallas kernels, gather_rows(): pl.pallas_call(functools.partial(gather_kernel, dp_size, line_size, ROW_F...  91.8 us
    pallas_call x1, Pallas kernels, scatter_rows(): pl.pallas_call(functools.partial(scatter_kernel, dp_size, line_size), out...  37.1 us
    pallas_call x1, Pallas kernels, head_sum(): pl.pallas_call(heads_kernel, out_shape=jax.ShapeDtypeStruct((2, 2, half,...  22.2 us
    psum x1, blocking collectives, local(): counts = lax.psum(onehot, ('dp', 'fsdp'))  20.8 us
    dot_general x2, local copies, waits for them, and re-layouts, local(): jnp.dot(stacked, gathered[k], preferred_element_type=jnp.float32)  7.99 us
    dot_general x3, matrix products, local(): jnp.dot(stacked, gathered[k], preferred_element_type=jnp.float32)  7.9 us
    unnamed x25, local copies, waits for them, and re-layouts  7.42 us
    slice x1, local copies, waits for them, and re-layouts, local(): out_rows = gathered[3]  5.8 us

profile of v1, /device:TPU:0, one launch (start us, length us, event | category | flops | bytes accessed | tf_op | source)
XLA Modules:
  0.0 235.9 jit_solution(18213594735206388735)
XLA Ops:
  0.7 0.9 bitcast_convert_fusion
  1.6 1.5 convert_reduce_fusion
  3.2 1.8 fusion.5
  4.9 1.1 pad_maximum_fusion.1.blocks_ref
  6.0 0.7 copy.24.thin_ref
  6.7 91.8 %shard_map.138 = (bf16[4,8,304,384]{3,2,1,0:T(8,128)(2,1)}, bf16[8,304,64]{2,1,0:T(8,128)(2,1)}) custom-call(bf16[4,304,384]{2,1,0:T(8,128)(2,1)} %pad_maximum_fusion.1.blocks_ref, bf16[304,64]{1,0:T(8,128)(2,1)} %copy.24.thin_ref), custom_call_target="tpu_custom_call" | custom-call | tf_op jit(solution)/shard_map/pallas_call | solution.py:228
  98.6 5.8 %fusion.63 = (bf16[1,8,304,384]{3,2,1,0:T(8,128)(2,1)S(1)}, bf16[1,8,304,384]{3,2,1,0:T(8,128)(2,1)}, bf16[1,8,304,384]{3,2,1,0:T(8,128)(2,1)}, bf16[1,8,304,384]{3,2,1,0:T(8,128)(2,1)}) fusion(bf16[4,8,304,384]{3,2,1,0:T(8,128)(2,1)} %get-tuple-element.6), kind=kLoop, calls=%fused_computation.109 | loop fusion | bytes 14942208 | tf_op jit(solution)/shard_map/slice | solution.py:432
  104.4 4.0 %copy.28 = bf16[384,2432]{1,0:T(8,128)(2,1)} copy(bf16[384,2432]{0,1:T(8,128)(2,1)} %bitcast.140) | data formatting | bytes 3735552 | tf_op jit(solution)/shard_map/dot_general | solution.py:434
  108.5 2.3 multiply_reduce_fusion.2
  110.9 3.9 %copy.27 = bf16[384,2432]{1,0:T(8,128)(2,1)} copy(bf16[384,2432]{0,1:T(8,128)(2,1)} %bitcast.139) | data formatting | bytes 3735552 | tf_op jit(solution)/shard_map/dot_general | solution.py:434
  114.8 3.1 %multiply_reduce_fusion.3 = (f32[2,128,6]{1,2,0:T(8,128)S(1)}, f32[2,128,6,64]{1,3,2,0:T(8,128)}) fusion(bf16[6,64,2432,1]{2,1,0,3:T(8,128)(2,1)} %bitcast.147, bf16[1,2,128,2432]{3,2,1,0:T(8,128)(2,1)S(1)} %copy-done, f32[2,2432]{1,0:T(2,128)S(1)} %get-tuple-element.30, f32[2,2432]{1,0:T(2,128)S(1)} %get-tuple-element.31, ...), kind=kOutput, calls=%fused_computation.56 | convolution fusion | flops 482081280 | bytes 3553280 | tf_op jit(solution)/shard_map/dot_general | solution.py:434
  117.9 4.7 %copy.26 = bf16[1,2,333,6,128]{2,4,3,1,0:T(8,128)(2,1)} copy(bf16[1,2,333,6,128]{4,1,3,2,0:T(2,128)(2,1)} %param.12) | data formatting | bytes 2045952 | tf_op args[1]
  122.6 1.2 fusion.24
  123.8 1.2 fusion.25
  125.0 3.3 %fusion.3 = (f32[2,6,128]{2,1,0:T(8,128)S(1)}, f32[2,6,128,461]{2,3,1,0:T(8,128)}) fusion(bf16[2,333,6,64]{1,3,2,0:T(8,128)(2,1)S(1)} %fusion.25, bf16[2,128,6,64]{1,3,2,0:T(8,128)(2,1)S(1)} %multiply_convert_fusion.1, f32[2,128,6,64]{1,3,2,0:T(8,128)} %get-tuple-element.35, f32[2,128,6]{1,2,0:T(8,128)S(1)} %add_rsqrt_fusion.2), kind=kOutput, calls=%fused_computation.12 | convolution fusion | flops 93663744 | bytes 3945984 | tf_op jit(solution)/shard_map/bqhe,bkhe->bhqk/dot_general | solution.py:78
  128.4 3.9 %copy.25 = bf16[2432,384]{0,1:T(8,128)(2,1)} copy(bf16[2432,384]{1,0:T(8,128)(2,1)} %bitcast.138) | data formatting | bytes 3735552 | tf_op jit(solution)/shard_map/squeeze | solution.py:434
  132.3 2.5 %convolution_convert_fusion.1 = bf16[2,128,6,64]{1,3,2,0:T(8,128)(2,1)S(1)} fusion(bf16[6,64,2432,1]{2,1,0,3:T(8,128)(2,1)} %bitcast.145, bf16[1,2,128,2432]{3,2,1,0:T(8,128)(2,1)S(1)} %copy-done, f32[2,2432]{1,0:T(2,128)S(1)} %get-tuple-element.30, f32[2,2432]{1,0:T(2,128)S(1)} %get-tuple-element.31, f32[2,128]{1,0:T(2,128)S(1)} %add_rsqrt_fusion.4, ...), kind=kOutput, calls=%fused_computation.44 | convolution fusion | flops 481984512 | bytes 3350528 | tf_op jit(solution)/shard_map/dot_general | solution.py:434
  135.0 0.7 fusion.26
  135.8 22.2 %shard_map.139 = bf16[2,2,64,2432]{3,2,1,0:T(8,128)(2,1)S(1)} custom-call(bf16[2,128,384]{2,1,0:T(8,128)(2,1)S(1)} %copy.29.attended_ref, bf16[2432,384]{1,0:T(8,128)(2,1)S(1)} %bitcast.136), custom_call_target="tpu_custom_call" | custom-call | tf_op jit(solution)/shard_map/pallas_call | solution.py:388
  158.0 1.8 fusion.61
  160.3 0.9 copy-done.1
  161.3 0.9 fusion.22
  163.8 20.8 %psum.7 = f32[4]{0:T(128)S(1)} all-reduce(f32[4]{0:T(128)S(1)} %compare_convert_fusion), channel_id=1, replica_groups=mesh['dp'=2,'tp'=4,'fsdp'=4] {'dp','fsdp'}, use_global_device_ids=true, to_apply=%region_9.0 | all-reduce | flops 4 | bytes 32 | tf_op jit(solution)/shard_map/psum | solution.py:447
  186.6 0.9 fusion.60
  187.6 1.0 multiply_convert_fusion
  188.7 0.7 convolution_convert_fusion
  190.0 1.5 pad_maximum_fusion
  191.5 3.2 %copy.33 = bf16[2432,448]{1,0:T(8,128)(2,1)S(1)} copy(bf16[2432,448]{0,1:T(8,128)(2,1)} %pad_maximum_fusion) | data formatting | bytes 4358144 | tf_op jit(solution)/shard_map/concatenate | solution.py:465
  194.7 37.1 %shard_map.140 = f32[304,448]{1,0:T(8,128)S(1)} custom-call(bf16[8,304,448]{2,1,0:T(8,128)(2,1)S(1)} %bitcast.135), custom_call_target="tpu_custom_call" | custom-call | tf_op jit(solution)/shard_map/pallas_call | solution.py:322
  231.9 0.8 slice.68
  232.7 0.8 copy.34
  233.5 0.6 fusion.46
  (41 shorter events, 2.6 us)
Async XLA Ops:
  0.6 4.3 %copy-start.4 = (bf16[304,3,384]{2,0,1:T(8,128)(2,1)S(1)}, bf16[304,3,384]{2,0,1:T(8,128)(2,1)}, u32[]{:S(2)}) copy-start(bf16[304,3,384]{2,0,1:T(8,128)(2,1)} %param.19) | copy-start | bytes 2101252
  0.6 4.3 %copy-start.6 = (bf16[304,384]{1,0:T(8,128)(2,1)S(1)}, bf16[304,384]{1,0:T(8,128)(2,1)}, u32[]{:S(2)}) copy-start(bf16[304,384]{1,0:T(8,128)(2,1)} %param.20) | copy-start | bytes 700420
  0.7 5.4 %copy-start.10 = (bf16[304,64]{0,1:T(8,128)(2,1)S(1)}, bf16[304,64]{0,1:T(8,128)(2,1)}, u32[]{:S(2)}) copy-start(bf16[304,64]{0,1:T(8,128)(2,1)} %param.21) | copy-start | bytes 116740
  104.4 4.0 %copy-start = (bf16[1,2,128,2432]{3,2,1,0:T(8,128)(2,1)S(1)}, bf16[1,2,128,2432]{3,2,1,0:T(8,128)(2,1)}, u32[]{:S(2)}) copy-start(bf16[1,2,128,2432]{3,2,1,0:T(8,128)(2,1)} %param.11) | copy-start | bytes 3735556
  132.3 2.5 %copy-start.2 = (bf16[1,2,333,6,128]{2,4,3,1,0:T(8,128)(2,1)S(1)}, bf16[1,2,333,6,128]{2,4,3,1,0:T(8,128)(2,1)}, u32[]{:S(2)}) copy-start(bf16[1,2,333,6,128]{2,4,3,1,0:T(8,128)(2,1)} %copy.26) | copy-start | bytes 3068932
  132.3 2.7 %copy-start.3 = (f32[2,6,128,461]{2,3,1,0:T(8,128)S(1)}, f32[2,6,128,461]{2,3,1,0:T(8,128)}, u32[]{:S(2)}) copy-start(f32[2,6,128,461]{2,3,1,0:T(8,128)} %get-tuple-element.37) | copy-start | bytes 8497156
  159.8 1.3 copy-start.1
  159.9 1.4 copy-start.5
  161.3 25.3 %copy-start.7 = (f32[1,128,64]{1,2,0:T(8,128)S(1)}, f32[1,128,64]{1,2,0:T(8,128)}, u32[]{:S(2)}) copy-start(f32[1,128,64]{1,2,0:T(8,128)} %param.15) | copy-start | bytes 98308
  161.3 25.3 %copy-start.8 = (f32[1,128,64]{1,2,0:T(8,128)S(1)}, f32[1,128,64]{1,2,0:T(8,128)}, u32[]{:S(2)}) copy-start(f32[1,128,64]{1,2,0:T(8,128)} %param.14) | copy-start | bytes 98308
  186.6 0.9 copy-start.9

commit v2 on v1

--- a/solution.py
+++ b/solution.py
@@ -9,7 +9,6 @@
 from jax.sharding import PartitionSpec as P
 
 STEPS = 10
-GROUPS = 4
 ROW_FIRST = (3, 4)
 
 
@@ -63,27 +62,55 @@
     return (following, log_density, slope)
 
 
-def attend(projected, text_pair):
-    head_width = projected.shape[-1]
-    query = rms_norm(projected[:, :, 0])
-    key_image = rms_norm(projected[:, :, 1])
-    key_text = rms_norm(text_pair[..., :head_width].astype(jnp.float32))
-    query_half = query.astype(jnp.bfloat16)
-    key_all = jnp.concatenate([key_image.astype(jnp.bfloat16), key_text.astype(jnp.bfloat16)], 1)
-    value_all = jnp.concatenate(
-        [projected[:, :, 2].astype(jnp.bfloat16), text_pair[..., head_width:]], 1
-    )
-    score_scale = 1.0 / math.sqrt(head_width)
-    scores = (
-        jnp.einsum("bqhe,bkhe->bhqk", query_half, key_all, preferred_element_type=jnp.float32)
-        * score_scale
-    )
-    exponent = jnp.exp(scores)
-    attention = exponent / jnp.sum(exponent, axis=-1, keepdims=True)
-    attention_half = attention.astype(jnp.bfloat16)
-    return jnp.einsum(
-        "bhqk,bkhe->bqhe", attention_half, value_all, preferred_element_type=jnp.float32
-    ).astype(jnp.bfloat16)
+def attend_kernel(rows_ref, w_ref, text_ref, out_ref):
+    passes, heads, _, pair = text_ref.shape
+    width = pair // 2
+    tokens = out_ref.shape[1]
+    query_all, key_all, value_all = (
+        jnp.dot(rows_ref[...], w_ref[k], preferred_element_type=jnp.float32) for k in range(3)
+    )
+    value_all = value_all.astype(jnp.bfloat16)
+    score_scale = 1.0 / math.sqrt(width)
+    across = (((1,), (1,)), ((), ()))
+    for which in range(passes):
+        here = slice(which * tokens, (which + 1) * tokens)
+        outs = []
+        for head in range(heads):
+            lanes = slice(head * width, (head + 1) * width)
+            query = rms_norm(query_all[here, lanes]).astype(jnp.bfloat16)
+            key_image = rms_norm(key_all[here, lanes]).astype(jnp.bfloat16)
+            text = text_ref[which, head]
+            key_text = rms_norm(text[:, :width].astype(jnp.float32)).astype(jnp.bfloat16)
+            image, words = (
+                jnp.exp(
+                    lax.dot_general(query, key, across, preferred_element_type=jnp.float32)
+                    * score_scale
+                )
+                for key in (key_image, key_text)
+            )
+            total = jnp.sum(image, axis=-1, keepdims=True) + jnp.sum(words, axis=-1, keepdims=True)
+            from_image = jnp.dot(
+                (image / total).astype(jnp.bfloat16),
+                value_all[here, lanes],
+                preferred_element_type=jnp.float32,
+            )
+            from_text = jnp.dot(
+                (words / total).astype(jnp.bfloat16), text, preferred_element_type=jnp.float32
+            )
+            outs.append((from_image + from_text[:, width:]).astype(jnp.bfloat16))
+        out_ref[which] = jnp.concatenate(outs, 1)
+
+
+def attend(stacked, w_blocks, text_pair):
+    passes, _, heads, pair = text_pair.shape
+    tokens = stacked.shape[0] // passes
+    return pl.pallas_call(
+        attend_kernel,
+        out_shape=jax.ShapeDtypeStruct((passes, tokens, heads * pair // 2), jnp.bfloat16),
+        in_specs=[pl.BlockSpec(memory_space=pltpu.VMEM)] * 3,
+        out_specs=pl.BlockSpec(memory_space=pltpu.VMEM),
+        compiler_params=pltpu.CompilerParams(vmem_limit_bytes=48 * 1024 * 1024),
+    )(stacked, w_blocks, jnp.transpose(text_pair, (0, 2, 1, 3)))
 
 
 def greet(peers):
@@ -416,9 +443,7 @@
 ):
     row_count = hidden.shape[2]
     model_width = hidden.shape[3]
-    heads = text_kv.shape[3]
-    head_width = text_kv.shape[4] // 2
-    head_columns = heads * head_width
+    head_columns = text_kv.shape[3] * text_kv.shape[4] // 2
     residual = hidden[0].astype(jnp.float32)
     mod_values = mods[0].astype(jnp.float32)
     normed, inverse = layer_norm(residual)
@@ -426,16 +451,17 @@
     stacked = modulated.reshape(2 * row_count, model_width)
     dp_size, line_size = lax.axis_size("dp"), lax.axis_size("fsdp")
     blocks = jnp.concatenate([jnp.swapaxes(w_qkv, 0, 1), w_out[None]], 0)
-    gathered, final_rows = gather_rows(blocks, w_final, dp_size, line_size)
+    patch = w_final.shape[1]
+    group_column = jnp.broadcast_to(
+        group_id[:, None].astype(jnp.bfloat16), (w_final.shape[0], patch)
+    )
+    thin = jnp.concatenate([w_final, group_column], 1)
+    gathered, all_thin = gather_rows(blocks, thin, dp_size, line_size)
     gathered = gathered.reshape(4, model_width, head_columns)
-    final_rows = final_rows.reshape(model_width, -1)
+    groups = all_thin[:, 0, patch].astype(jnp.int32)
+    final_rows = all_thin.reshape(model_width, -1)[:, :patch]
     out_rows = gathered[3]
-    projected = jnp.stack(
-        [jnp.dot(stacked, gathered[k], preferred_element_type=jnp.float32) for k in range(3)], 1
-    )
-    projected = projected.reshape(2, row_count, 3, heads, head_width)
-    attended = attend(projected, text_kv[0])
-    attended_flat = attended.reshape(2, row_count, head_columns)
+    attended_flat = attend(stacked, gathered, text_kv[0])
     partial_sum = head_sum(attended_flat, out_rows).astype(jnp.float32)
     updated = residual + mod_values[:, 2:3] * partial_sum
     final_normed, final_inverse = layer_norm(updated)
@@ -443,9 +469,7 @@
     velocity = jnp.einsum("brd,dp->brp", readout, final_rows, preferred_element_type=jnp.float32)
     guided = velocity[1] + guidance * (velocity[0] - velocity[1])
     following, log_density, slope = transition(latents[0], noise[0], guided, step_index[0], STEPS)
-    onehot = (group_id[0] == jnp.arange(GROUPS, dtype=jnp.int32)).astype(jnp.float32)
-    counts = lax.psum(onehot, ("dp", "fsdp"))
-    members = jnp.sum(onehot * counts)
+    members = jnp.sum((groups == group_id[0]).astype(jnp.float32))
     sample_weight = loss_scale * advantages[0] / members
     upstream_velocity = sample_weight * slope
     velocity_grad = jnp.stack(

time: 237 us -> 195 us (0.82)
  blocking collectives: 20.8 us -> 0 us
  local copies, waits for them, and re-layouts: 29.6 us -> 9.68 us
  Pallas kernels: 151 us -> 164 us
  matrix products: 15 us -> 3.42 us
    psum x1 -> x0, blocking collectives: 20.8 us -> none  [local(): counts = lax.psum(onehot, ('dp', 'fsdp'))]
    dot_general x5 -> x0, matrix products: 11.9 us -> none  [the longest x3 7.9 us: local(): jnp.dot(stacked, gathered[k], preferred_element_type=jnp.float32)]
    pallas_call x0 -> x1, Pallas kernels: none -> 9.5 us  [attend(): pl.pallas_call(attend_kernel, out_shape=jax.ShapeDtypeStruct((passes, tok...]
    dot_general x2 -> x0, local copies, waits for them, and re-layouts: 7.99 us -> none  [local(): jnp.dot(stacked, gathered[k], preferred_element_type=jnp.float32)]
    unnamed x25 -> x21, local copies, waits for them, and re-layouts: 7.42 us -> 3.31 us
    slice x1, local copies, waits for them, and re-layouts: 5.8 us -> 1.7 us  [local(): out_rows = gathered[3]]
    squeeze x1 -> x0, local copies, waits for them, and re-layouts: 3.91 us -> none  [local(): gathered[k]]
    pallas_call x1, Pallas kernels: 37.1 us -> 40.5 us  [scatter_rows(): pl.pallas_call(functools.partial(scatter_kernel, dp_size, line_size), out...]
where the time goes in v2:
time: 195 us
  Pallas kernels  164 us (84%)
  other arithmetic  11.9 us (6%)
  local copies, waits for them, and re-layouts  9.68 us (5%)
  between operations  5.65 us (3%)
  matrix products  3.42 us (2%)
    pallas_call x1, Pallas kernels, gather_rows(): pl.pallas_call(functools.partial(gather_kernel, dp_size, line_size, ROW_F...  91.8 us
    pallas_call x1, Pallas kernels, scatter_rows(): pl.pallas_call(functools.partial(scatter_kernel, dp_size, line_size), out...  40.5 us
    pallas_call x1, Pallas kernels, head_sum(): pl.pallas_call(heads_kernel, out_shape=jax.ShapeDtypeStruct((2, 2, half,...  22.2 us
    pallas_call x1, Pallas kernels, attend(): pl.pallas_call(attend_kernel, out_shape=jax.ShapeDtypeStruct((passes, tok...  9.5 us

profile of v2, /device:TPU:0, one launch (start us, length us, event | category | flops | bytes accessed | tf_op | source)
XLA Modules:
  0.0 194.7 jit_solution(6036837357925993462)
XLA Ops:
  0.6 0.0 copy-start
  0.6 0.9 bitcast_convert_fusion
  1.6 0.0 copy-start.8
  1.6 0.0 copy-start.3
  1.6 1.6 convert_reduce_fusion
  3.2 1.8 fusion.6
  5.0 0.6 fusion.3.rows_ref
  6.3 0.1 copy.21
  6.4 0.7 concatenate.10.thin_ref
  7.1 2.0 %pad_maximum_fusion.1.blocks_ref = bf16[4,304,384]{2,1,0:T(8,128)(2,1)} fusion(bf16[1,304,384]{2,1,0:T(8,128)(2,1)} %bitcast.134, bf16[3,304,384]{2,1,0:T(8,128)(2,1)S(1)} %bitcast.131), kind=kLoop, calls=%fused_computation.29 | loop fusion | flops 466944 | bytes 1867776 | tf_op jit(solution)/shard_map/concatenate | solution.py:453
  9.1 91.8 %shard_map.138 = (bf16[4,8,304,384]{3,2,1,0:T(8,128)(2,1)}, bf16[8,304,128]{2,1,0:T(8,128)(2,1)}) custom-call(bf16[4,304,384]{2,1,0:T(8,128)(2,1)} %pad_maximum_fusion.1.blocks_ref, bf16[304,128]{1,0:T(8,128)(2,1)} %concatenate.10.thin_ref), custom_call_target="tpu_custom_call" | custom-call | tf_op jit(solution)/shard_map/pallas_call | solution.py:255
  100.9 1.4 copy.30
  102.3 9.5 %shard_map.139.attended_ref = bf16[2,128,384]{2,1,0:T(8,128)(2,1)S(1)} custom-call(bf16[256,2432]{1,0:T(8,128)(2,1)S(1)} %fusion.3.rows_ref, bf16[4,2432,384]{2,1,0:T(8,128)(2,1)} %bitcast.130, bf16[2,6,333,128]{3,2,1,0:T(8,128)(2,1)S(1)} %bitcast.129), custom_call_target="tpu_custom_call" | custom-call | tf_op jit(solution)/shard_map/pallas_call | solution.py:107
  111.8 1.7 slice.43
  113.5 22.2 %shard_map.140 = bf16[2,2,64,2432]{3,2,1,0:T(8,128)(2,1)S(1)} custom-call(bf16[2,128,384]{2,1,0:T(8,128)(2,1)S(1)} %shard_map.139.attended_ref, bf16[2432,384]{1,0:T(8,128)(2,1)S(1)} %bitcast.128), custom_call_target="tpu_custom_call" | custom-call | tf_op jit(solution)/shard_map/pallas_call | solution.py:415
  135.7 0.5 fusion.7
  136.2 0.7 multiply_reduce_fusion.1
  136.9 0.0 copy-start.5
  136.9 0.0 copy-start.6
  136.9 0.9 add_convert_fusion
  137.9 1.0 copy-done.1
  138.9 0.5 fusion.13
  140.4 0.7 fusion.26
  142.5 1.2 fusion.30
  143.7 1.4 fusion
  145.1 0.3 fusion.1
  145.5 1.5 pad_maximum_fusion
  147.0 3.2 %copy.25 = bf16[2432,448]{1,0:T(8,128)(2,1)S(1)} copy(bf16[2432,448]{0,1:T(8,128)(2,1)} %pad_maximum_fusion) | data formatting | bytes 4358144 | tf_op jit(solution)/shard_map/concatenate | solution.py:489
  150.2 40.5 %shard_map.141 = f32[304,448]{1,0:T(8,128)S(1)} custom-call(bf16[8,304,448]{2,1,0:T(8,128)(2,1)S(1)} %bitcast.127), custom_call_target="tpu_custom_call" | custom-call | tf_op jit(solution)/shard_map/pallas_call | solution.py:349
  190.7 0.8 slice.50
  191.5 0.8 copy.26
  192.3 0.6 fusion.23
  (21 shorter events, 0.1 us)
Async XLA Ops:
  0.6 4.4 %copy-start = (bf16[1,2,128,2432]{3,2,1,0:T(8,128)(2,1)S(1)}, bf16[1,2,128,2432]{3,2,1,0:T(8,128)(2,1)}, u32[]{:S(2)}) copy-start(bf16[1,2,128,2432]{3,2,1,0:T(8,128)(2,1)} %param.11) | copy-start | bytes 3735556
  1.6 4.7 %copy-start.8 = (bf16[304,64]{0,1:T(8,128)(2,1)S(1)}, bf16[304,64]{0,1:T(8,128)(2,1)}, u32[]{:S(2)}) copy-start(bf16[304,64]{0,1:T(8,128)(2,1)} %param.21) | copy-start | bytes 116740
  1.6 5.4 %copy-start.3 = (bf16[304,3,384]{2,0,1:T(8,128)(2,1)S(1)}, bf16[304,3,384]{2,0,1:T(8,128)(2,1)}, u32[]{:S(2)}) copy-start(bf16[304,3,384]{2,0,1:T(8,128)(2,1)} %param.19) | copy-start | bytes 2101252
  136.9 2.0 %copy-start.4 = (bf16[8,304,128]{2,1,0:T(8,128)(2,1)S(1)}, bf16[8,304,128]{2,1,0:T(8,128)(2,1)}, u32[]{:S(2)}) copy-start(bf16[8,304,128]{2,1,0:T(8,128)(2,1)} %get-tuple-element.7) | copy-start | bytes 1867780
  136.9 5.5 %copy-start.5 = (f32[1,128,64]{1,2,0:T(8,128)S(1)}, f32[1,128,64]{1,2,0:T(8,128)}, u32[]{:S(2)}) copy-start(f32[1,128,64]{1,2,0:T(8,128)} %param.15) | copy-start | bytes 98308
  136.9 5.5 %copy-start.6 = (f32[1,128,64]{1,2,0:T(8,128)S(1)}, f32[1,128,64]{1,2,0:T(8,128)}, u32[]{:S(2)}) copy-start(f32[1,128,64]{1,2,0:T(8,128)} %param.14) | copy-start | bytes 98308
  137.9 1.0 copy-start.1
  142.5 1.2 copy-start.7
  143.7 1.4 copy-start.2

commit v3 on v2

--- a/solution.py
+++ b/solution.py
@@ -9,7 +9,8 @@
 from jax.sharding import PartitionSpec as P
 
 STEPS = 10
-ROW_FIRST = (3, 4)
+ROW_FIRST = (4, 5)
+NARROW = 128
 
 
 eps_norm = 1e-06
@@ -45,21 +46,6 @@
     time_next = time_shift * level_next / (1.0 + (time_shift - 1.0) * level_next)
     noise_scale = noise_level * jnp.sqrt(time_now / (1.0 - time_now))
     return (time_now, time_now - time_next, noise_scale)
-
-
-def transition(latent, noise_draw, velocity, sample_step, step_count):
-    time_now, step_size, noise_scale = plan(sample_step, step_count)
-    spread = noise_scale * jnp.sqrt(step_size)
-    drift_velocity = 1.0 + noise_scale * noise_scale * (1.0 - time_now) / (2.0 * time_now)
-    drift_latent = noise_scale * noise_scale / (2.0 * time_now)
-    centre = latent - step_size * (drift_velocity * velocity + drift_latent * latent)
-    following = centre + spread * noise_draw
-    offset = following - centre
-    log_density = jnp.mean(
-        -offset * offset / (2.0 * spread * spread) - jnp.log(spread) - 0.5 * math.log(2.0 * math.pi)
-    )
-    slope = step_size * drift_velocity * offset / (spread * spread * offset.size)
-    return (following, log_density, slope)
 
 
 def attend_kernel(rows_ref, w_ref, text_ref, out_ref):
@@ -152,13 +138,22 @@
 ):
     row, spot, across, sides, has_side, peers = around(dp_size, line_size)
     count = blocks_ref.shape[0]
+    cut = blocks_ref.shape[2] - NARROW
     me = row * line_size + spot
 
     def mine(k):
-        return blocks_ref.at[k] if k < count else thin_ref
+        if k > count:
+            return thin_ref
+        if k == count:
+            return blocks_ref.at[count - 1, :, pl.ds(cut, NARROW)]
+        return blocks_ref.at[k, :, pl.ds(0, cut)] if k == count - 1 else blocks_ref.at[k]
 
     def slot(k, which):
-        return all_ref.at[k, which] if k < count else all_thin_ref.at[which]
+        if k > count:
+            return all_thin_ref.at[which]
+        if k == count:
+            return all_ref.at[count - 1, which, :, pl.ds(cut, NARROW)]
+        return all_ref.at[k, which, :, pl.ds(0, cut)] if k == count - 1 else all_ref.at[k, which]
 
     def along(k, which, side, own):
         src = mine(k) if own else slot(k, which)
@@ -181,7 +176,7 @@
         def _():
             action()
 
-    order = list(range(count + 1))
+    order = list(range(count + 2))
     greet(peers)
     keep = [pltpu.make_async_copy(mine(k), slot(k, me), local_sem.at[k]) for k in order]
     started = []
@@ -249,7 +244,7 @@
 
 
 def gather_rows(blocks, thin, dp_size, line_size):
-    kinds = blocks.shape[0] + 1
+    kinds = blocks.shape[0] + 2
     total = dp_size * line_size
     dma = pltpu.SemaphoreType.DMA
     return pl.pallas_call(
@@ -438,6 +433,80 @@
     )
 
 
+def middle_kernel(
+    scalar_ref, hidden_ref, sum_ref, mods_ref, final_ref, latent_ref, noise_ref, attended_ref,
+    next_ref, offset_ref, parts_ref, normed_ref, readout_ref, grad_ref,
+):
+    spread, step_size, drift_velocity, drift_latent, sample_weight = (
+        scalar_ref[k] for k in range(5)
+    )
+    passes, tokens, _ = hidden_ref.shape
+    inverses, velocity = [], []
+    for which in range(passes):
+        updated = hidden_ref[which].astype(jnp.float32) + mods_ref[which, 2:3] * sum_ref[
+            which
+        ].astype(jnp.float32)
+        normed, inverse = layer_norm(updated)
+        normed_ref[which] = normed
+        inverses.append(inverse)
+        readout = (normed * (1.0 + mods_ref[which, 4:5]) + mods_ref[which, 3:4]).astype(
+            jnp.bfloat16
+        )
+        readout_ref[which * tokens : (which + 1) * tokens] = readout
+        velocity.append(jnp.dot(readout, final_ref[...], preferred_element_type=jnp.float32))
+    guided = velocity[1] + guidance * (velocity[0] - velocity[1])
+    latent = latent_ref[...]
+    centre = latent - step_size * (drift_velocity * guided + drift_latent * latent)
+    following = centre + spread * noise_ref[...]
+    offset = following - centre
+    next_ref[...] = following
+    offset_ref[...] = offset
+    slope = step_size * drift_velocity * offset / (spread * spread * offset.size)
+    upstream = sample_weight * slope
+    grads = [
+        (factor * upstream).astype(jnp.bfloat16) for factor in (guidance, 1.0 - guidance)
+    ]
+    for which in range(passes):
+        readout_grad = lax.dot_general(
+            grads[which], final_ref[...], (((1,), (1,)), ((), ())),
+            preferred_element_type=jnp.float32,
+        )
+        updated_grad = layer_norm_back(
+            readout_grad * (1.0 + mods_ref[which, 4:5]), normed_ref[which], inverses[which]
+        )
+        grad_ref[which * tokens : (which + 1) * tokens] = (
+            mods_ref[which, 2:3] * updated_grad
+        ).astype(jnp.bfloat16)
+    columns = attended_ref.shape[1]
+    parts_ref[:, :columns] = contract_rows(grad_ref[...], attended_ref[...]).astype(jnp.bfloat16)
+    parts_ref[:, columns:] = contract_rows(
+        readout_ref[...], jnp.concatenate(grads, 0)
+    ).astype(jnp.bfloat16)
+
+
+def middle(scalars, hidden, total, mods, final_rows, latent, noise, attended):
+    passes, tokens, model_width = hidden.shape
+    whole = pl.BlockSpec(memory_space=pltpu.VMEM)
+    return pl.pallas_call(
+        middle_kernel,
+        out_shape=(
+            jax.ShapeDtypeStruct(latent.shape, jnp.float32),
+            jax.ShapeDtypeStruct(latent.shape, jnp.float32),
+            jax.ShapeDtypeStruct(
+                (model_width, attended.shape[1] + final_rows.shape[1]), jnp.bfloat16
+            ),
+        ),
+        in_specs=[pl.BlockSpec(memory_space=pltpu.SMEM)] + [whole] * 7,
+        out_specs=(whole,) * 3,
+        scratch_shapes=[
+            pltpu.VMEM((passes, tokens, model_width), jnp.float32),
+            pltpu.VMEM((passes * tokens, model_width), jnp.bfloat16),
+            pltpu.VMEM((passes * tokens, model_width), jnp.bfloat16),
+        ],
+        compiler_params=pltpu.CompilerParams(vmem_limit_bytes=48 * 1024 * 1024),
+    )(scalars, hidden, total, mods, final_rows, latent, noise, attended)
+
+
 def local(
     hidden, text_kv, mods, latents, noise, step_index, group_id, advantages, w_qkv, w_out, w_final
 ):
@@ -462,36 +531,22 @@
     final_rows = all_thin.reshape(model_width, -1)[:, :patch]
     out_rows = gathered[3]
     attended_flat = attend(stacked, gathered, text_kv[0])
-    partial_sum = head_sum(attended_flat, out_rows).astype(jnp.float32)
-    updated = residual + mod_values[:, 2:3] * partial_sum
-    final_normed, final_inverse = layer_norm(updated)
-    readout = (final_normed * (1.0 + mod_values[:, 4:5]) + mod_values[:, 3:4]).astype(jnp.bfloat16)
-    velocity = jnp.einsum("brd,dp->brp", readout, final_rows, preferred_element_type=jnp.float32)
-    guided = velocity[1] + guidance * (velocity[0] - velocity[1])
-    following, log_density, slope = transition(latents[0], noise[0], guided, step_index[0], STEPS)
+    total = head_sum(attended_flat, out_rows)
+    time_now, step_size, noise_scale = plan(step_index[0], STEPS)
+    spread = noise_scale * jnp.sqrt(step_size)
+    drift_velocity = 1.0 + noise_scale * noise_scale * (1.0 - time_now) / (2.0 * time_now)
+    drift_latent = noise_scale * noise_scale / (2.0 * time_now)
     members = jnp.sum((groups == group_id[0]).astype(jnp.float32))
     sample_weight = loss_scale * advantages[0] / members
-    upstream_velocity = sample_weight * slope
-    velocity_grad = jnp.stack(
-        [guidance * upstream_velocity, (1.0 - guidance) * upstream_velocity], 0
-    ).astype(jnp.bfloat16)
-    readout_grad = jnp.einsum(
-        "brp,dp->brd", velocity_grad, final_rows, preferred_element_type=jnp.float32
-    )
-    updated_grad = layer_norm_back(
-        readout_grad * (1.0 + mod_values[:, 4:5]), final_normed, final_inverse
-    )
-    partial_grad = (mod_values[:, 2:3] * updated_grad).astype(jnp.bfloat16)
-    readout_flat = readout.reshape(2 * row_count, model_width)
-    velocity_flat = velocity_grad.reshape(2 * row_count, -1)
-    partial_flat = partial_grad.reshape(2 * row_count, model_width)
-    attended_rows = attended_flat.reshape(2 * row_count, head_columns)
-    parts = jnp.concatenate(
-        [
-            contract_rows(partial_flat, attended_rows).astype(jnp.bfloat16),
-            contract_rows(readout_flat, velocity_flat).astype(jnp.bfloat16),
-        ],
-        1,
+    scalars = jnp.stack([spread, step_size, drift_velocity, drift_latent, sample_weight])
+    following, offset, parts = middle(
+        scalars, hidden[0], total, mod_values, final_rows, latents[0], noise[0],
+        attended_flat.reshape(2 * row_count, head_columns),
+    )
+    log_density = jnp.mean(
+        -offset * offset / (2.0 * spread * spread)
+        - jnp.log(spread)
+        - 0.5 * math.log(2.0 * math.pi)
     )
     sums = scatter_rows(
         parts.reshape(dp_size * line_size, -1, parts.shape[1]), dp_size, line_size

time: 195 us -> 183 us (0.938)
  other arithmetic: 11.9 us -> 6.53 us
  Pallas kernels: 164 us -> 160 us
  matrix products: 3.42 us -> 0 us
    pallas_call x1, Pallas kernels: 91.8 us -> 83.7 us  [gather_rows(): pl.pallas_call(functools.partial(gather_kernel, dp_size, line_size, ROW_F...]
    pallas_call x0 -> x1, Pallas kernels: none -> 4.15 us  [middle(): pl.pallas_call(middle_kernel, out_shape=(jax.ShapeDtypeStruct(latent.shap...]
    dot_general x4 -> x0, matrix products: 3.42 us -> none  [the longest x2 1.74 us: contract_rows(): lax.dot_general(left, right, (((0,), (0,)), ((), ())), preferred_element_...]
    unnamed x21, local copies, waits for them, and re-layouts: 3.31 us -> 6.58 us
    concatenate x1 -> x0, local copies, waits for them, and re-layouts: 3.18 us -> none  [local(): jnp.concatenate([contract_rows(partial_flat, attended_rows).astype(jnp.bf...]
    reduce_sum x2 -> x1, other arithmetic: 2.45 us -> 0.47 us  [layer_norm(): jnp.mean(centred * centred, axis=-1, keepdims=True) + eps_norm]
where the time goes in v3:
time: 183 us; the launch traced here: 182 us
  Pallas kernels  160 us (87%)
  local copies, waits for them, and re-layouts  9.86 us (5%)
  other arithmetic  6.53 us (4%)
  between operations  5.58 us (3%)
    pallas_call x1, Pallas kernels, gather_rows(): pl.pallas_call(functools.partial(gather_kernel, dp_size, line_size, ROW_F...  83.7 us
    pallas_call x1, Pallas kernels, scatter_rows(): pl.pallas_call(functools.partial(scatter_kernel, dp_size, line_size), out...  40.7 us
    pallas_call x1, Pallas kernels, head_sum(): pl.pallas_call(heads_kernel, out_shape=jax.ShapeDtypeStruct((2, 2, half,...  22.2 us
    pallas_call x1, Pallas kernels, attend(): pl.pallas_call(attend_kernel, out_shape=jax.ShapeDtypeStruct((passes, tok...  9.5 us
    unnamed x21, local copies, waits for them, and re-layouts  6.58 us
    pallas_call x1, Pallas kernels, middle(): pl.pallas_call(middle_kernel, out_shape=(jax.ShapeDtypeStruct(latent.shap...  4.15 us

profile of v3, /device:TPU:0, one launch (start us, length us, event | category | flops | bytes accessed | tf_op | source)
XLA Modules:
  0.0 182.2 jit_solution(15650891800295677173)
XLA Ops:
  0.6 0.0 copy-start.6
  0.6 0.0 copy-start
  2.4 0.9 copy.22
  3.3 0.7 concatenate.7.thin_ref
  3.9 2.3 %pad_maximum_fusion.blocks_ref = bf16[4,304,384]{2,1,0:T(8,128)(2,1)} fusion(bf16[1,304,384]{2,1,0:T(8,128)(2,1)} %bitcast.63, bf16[3,304,384]{2,1,0:T(8,128)(2,1)} %bitcast.62), kind=kLoop, calls=%fused_computation.10 | loop fusion | flops 466944 | bytes 1867776 | tf_op jit(solution)/shard_map/concatenate | solution.py:522
  6.2 83.7 %shard_map.138 = (bf16[4,8,304,384]{3,2,1,0:T(8,128)(2,1)}, bf16[8,304,128]{2,1,0:T(8,128)(2,1)}) custom-call(bf16[4,304,384]{2,1,0:T(8,128)(2,1)} %pad_maximum_fusion.blocks_ref, bf16[304,128]{1,0:T(8,128)(2,1)} %concatenate.7.thin_ref), custom_call_target="tpu_custom_call" | custom-call | tf_op jit(solution)/shard_map/pallas_call | solution.py:250
  89.9 1.4 fusion.10
  92.5 0.1 stack.23.scalar_ref
  92.6 0.0 copy-done.6
  92.7 0.0 copy-done
  92.7 0.0 copy-start.5
  92.7 0.2 convert_reduce_fusion
  93.0 0.5 fusion.1
  93.5 0.6 fusion.5.rows_ref
  94.1 0.0 copy-done.5
  94.1 0.1 copy.35
  94.2 9.5 %shard_map.139.attended_ref = bf16[2,128,384]{2,1,0:T(8,128)(2,1)S(1)} custom-call(bf16[256,2432]{1,0:T(8,128)(2,1)S(1)} %fusion.5.rows_ref, bf16[4,2432,384]{2,1,0:T(8,128)(2,1)} %bitcast.61, bf16[2,6,333,128]{3,2,1,0:T(8,128)(2,1)S(1)} %bitcast.54), custom_call_target="tpu_custom_call" | custom-call | tf_op jit(solution)/shard_map/pallas_call | solution.py:93
  103.7 1.7 slice.25
  105.4 0.0 copy-start.1
  105.4 22.2 %shard_map.140 = bf16[2,2,64,2432]{3,2,1,0:T(8,128)(2,1)S(1)} custom-call(bf16[2,128,384]{2,1,0:T(8,128)(2,1)S(1)} %shard_map.139.attended_ref, bf16[2432,384]{1,0:T(8,128)(2,1)S(1)} %bitcast.52), custom_call_target="tpu_custom_call" | custom-call | tf_op jit(solution)/shard_map/pallas_call | solution.py:410
  127.6 0.8 copy.25
  128.5 1.5 copy.26
  130.0 0.0 copy-done.1
  130.0 0.8 copy-done.2
  130.8 4.2 %shard_map.141 = (f32[128,64]{1,0:T(8,128)S(1)}, f32[128,64]{1,0:T(8,128)S(1)}, bf16[2432,448]{1,0:T(8,128)(2,1)S(1)}) custom-call(f32[5]{0:T(128)S(1)} %stack.23.scalar_ref, bf16[2,128,2432]{2,1,0:T(8,128)(2,1)S(1)} %bitcast.51, bf16[2,128,2432]{2,1,0:T(8,128)(2,1)S(1)} %bitcast.53, f32[2,5,2432]{2,1,0:T(8,128)S(1)} %bitcast_convert_fusion.mods_ref, ...), custom_call_target="tpu_custom_call" | custom-call | tf_op jit(solution)/shard_map/pallas_call | solution.py:490
  135.0 0.0 copy-start.3
  135.0 40.7 %shard_map.142 = f32[304,448]{1,0:T(8,128)S(1)} custom-call(bf16[8,304,448]{2,1,0:T(8,128)(2,1)S(1)} %bitcast.55), custom_call_target="tpu_custom_call" | custom-call | tf_op jit(solution)/shard_map/pallas_call | solution.py:344
  175.8 0.8 slice.27
  176.6 0.0 copy-done.4
  176.6 0.8 copy.28
  177.4 1.5 fusion.9
  179.5 1.5 copy.27
  (9 shorter events, 0.1 us)
Async XLA Ops:
  0.6 92.0 %copy-start.6 = (bf16[1,2,5,2432]{3,1,2,0:T(2,128)(2,1)S(1)}, bf16[1,2,5,2432]{3,1,2,0:T(2,128)(2,1)}, u32[]{:S(2)}) copy-start(bf16[1,2,5,2432]{3,1,2,0:T(2,128)(2,1)} %param.13) | copy-start | bytes 145924
  0.6 92.1 %copy-start = (bf16[1,2,128,2432]{3,2,1,0:T(8,128)(2,1)S(1)}, bf16[1,2,128,2432]{3,2,1,0:T(8,128)(2,1)}, u32[]{:S(2)}) copy-start(bf16[1,2,128,2432]{3,2,1,0:T(8,128)(2,1)} %param.11) | copy-start | bytes 3735556
  92.7 1.4 copy-start.5
  105.4 24.6 %copy-start.1 = (bf16[8,304,128]{2,1,0:T(8,128)(2,1)S(1)}, bf16[8,304,128]{2,1,0:T(8,128)(2,1)}, u32[]{:S(2)}) copy-start(bf16[8,304,128]{2,1,0:T(8,128)(2,1)} %get-tuple-element.9) | copy-start | bytes 1867780
  130.0 0.8 copy-start.2
  135.0 40.8 %copy-start.3 = (f32[128,64]{1,0:T(8,128)}, f32[128,64]{1,0:T(8,128)S(1)}, u32[]{:S(2)}) copy-start(f32[128,64]{1,0:T(8,128)S(1)} %get-tuple-element.11) | copy-start | bytes 98308
  135.0 41.6 %copy-start.4 = (f32[128,64]{1,0:T(8,128)}, f32[128,64]{1,0:T(8,128)S(1)}, u32[]{:S(2)}) copy-start(f32[128,64]{1,0:T(8,128)S(1)} %get-tuple-element.12) | copy-start | bytes 98308

commit v4 on v3

--- a/solution.py
+++ b/solution.py
@@ -133,27 +133,28 @@
 
 
 def gather_kernel(
-    dp_size, line_size, row_first, blocks_ref, thin_ref, all_ref, all_thin_ref,
+    dp_size, line_size, row_first, blocks_ref, last_ref, thin_ref, all_ref, all_last_ref,
+    all_thin_ref,
     local_sem, recv_sem, line_sem, across_sem,
 ):
     row, spot, across, sides, has_side, peers = around(dp_size, line_size)
-    count = blocks_ref.shape[0]
-    cut = blocks_ref.shape[2] - NARROW
+    count = blocks_ref.shape[0] + 1
+    cut = last_ref.shape[1] - NARROW
     me = row * line_size + spot
 
     def mine(k):
         if k > count:
             return thin_ref
         if k == count:
-            return blocks_ref.at[count - 1, :, pl.ds(cut, NARROW)]
-        return blocks_ref.at[k, :, pl.ds(0, cut)] if k == count - 1 else blocks_ref.at[k]
+            return last_ref.at[:, pl.ds(cut, NARROW)]
+        return last_ref.at[:, pl.ds(0, cut)] if k == count - 1 else blocks_ref.at[k]
 
     def slot(k, which):
         if k > count:
             return all_thin_ref.at[which]
         if k == count:
-            return all_ref.at[count - 1, which, :, pl.ds(cut, NARROW)]
-        return all_ref.at[k, which, :, pl.ds(0, cut)] if k == count - 1 else all_ref.at[k, which]
+            return all_last_ref.at[which, :, pl.ds(cut, NARROW)]
+        return all_last_ref.at[which, :, pl.ds(0, cut)] if k == count - 1 else all_ref.at[k, which]
 
     def along(k, which, side, own):
         src = mine(k) if own else slot(k, which)
@@ -243,18 +244,19 @@
         when(condition, functools.partial(copy.wait_send))
 
 
-def gather_rows(blocks, thin, dp_size, line_size):
-    kinds = blocks.shape[0] + 2
+def gather_rows(blocks, last, thin, dp_size, line_size):
+    kinds = blocks.shape[0] + 3
     total = dp_size * line_size
     dma = pltpu.SemaphoreType.DMA
     return pl.pallas_call(
         functools.partial(gather_kernel, dp_size, line_size, ROW_FIRST),
         out_shape=(
             jax.ShapeDtypeStruct((blocks.shape[0], total) + blocks.shape[1:], blocks.dtype),
+            jax.ShapeDtypeStruct((total,) + last.shape, last.dtype),
             jax.ShapeDtypeStruct((total,) + thin.shape, thin.dtype),
         ),
-        in_specs=[pl.BlockSpec(memory_space=pl.ANY)] * 2,
-        out_specs=(pl.BlockSpec(memory_space=pl.ANY),) * 2,
+        in_specs=[pl.BlockSpec(memory_space=pl.ANY)] * 3,
+        out_specs=(pl.BlockSpec(memory_space=pl.ANY),) * 3,
         scratch_shapes=[
             dma((kinds,)),
             dma((kinds, total)),
@@ -262,11 +264,11 @@
             dma((max(dp_size - 1, 1), kinds, line_size)),
         ],
         compiler_params=pltpu.CompilerParams(collective_id=0, has_side_effects=True),
-    )(blocks, thin)
+    )(blocks, last, thin)
 
 
 def scatter_kernel(
-    dp_size, line_size, part_ref, out_ref, row_in, line_in, line_out,
+    dp_size, line_size, part_ref, wide_ref, thin_ref, row_in, line_in, line_out,
     row_send, row_recv, line_send, line_recv,
 ):
     row, spot, across, sides, has_side, peers = around(dp_size, line_size)
@@ -322,12 +324,17 @@
         @pl.when(stop > spot if side == 0 else stop < spot)
         def _():
             step(stop, side)
-    out_ref[...] = row_sum(spot)
+    value = row_sum(spot)
+    columns = wide_ref.shape[1]
+    wide_ref[...] = value[:, :columns]
+    thin_ref[...] = value[:, columns:]
     for side in (0, 1):
         @pl.when(has_side[1 - side])
         def _():
             along(spot, side).wait_recv()
-            out_ref[...] = out_ref[...] + line_in[side, spot].astype(jnp.float32)
+            extra = line_in[side, spot].astype(jnp.float32)
+            wide_ref[...] = wide_ref[...] + extra[:, :columns]
+            thin_ref[...] = thin_ref[...] + extra[:, columns:]
     for stop in range(line_size):
         for hop in range(dp_size - 1):
             over(stop, hop).wait_send()
@@ -337,15 +344,18 @@
             along(stop, side).wait_send()
 
 
-def scatter_rows(parts, dp_size, line_size):
+def scatter_rows(parts, columns, dp_size, line_size):
     block = parts.shape[1:]
     hops = max(dp_size - 1, 1)
     dma = pltpu.SemaphoreType.DMA
     return pl.pallas_call(
         functools.partial(scatter_kernel, dp_size, line_size),
-        out_shape=jax.ShapeDtypeStruct(block, jnp.float32),
+        out_shape=(
+            jax.ShapeDtypeStruct((block[0], columns), jnp.float32),
+            jax.ShapeDtypeStruct((block[0], block[1] - columns), jnp.float32),
+        ),
         in_specs=[pl.BlockSpec(memory_space=pltpu.VMEM)],
-        out_specs=pl.BlockSpec(memory_space=pltpu.VMEM),
+        out_specs=(pl.BlockSpec(memory_space=pltpu.VMEM),) * 2,
         scratch_shapes=[
             pltpu.VMEM((hops, line_size) + block, jnp.bfloat16),
             pltpu.VMEM((2, line_size) + block, jnp.bfloat16),
@@ -435,10 +445,10 @@
 
 def middle_kernel(
     scalar_ref, hidden_ref, sum_ref, mods_ref, final_ref, latent_ref, noise_ref, attended_ref,
-    next_ref, offset_ref, parts_ref, normed_ref, readout_ref, grad_ref,
+    next_ref, density_ref, parts_ref, normed_ref, readout_ref, grad_ref,
 ):
-    spread, step_size, drift_velocity, drift_latent, sample_weight = (
-        scalar_ref[k] for k in range(5)
+    spread, step_size, drift_velocity, drift_latent, sample_weight, level = (
+        scalar_ref[k] for k in range(6)
     )
     passes, tokens, _ = hidden_ref.shape
     inverses, velocity = [], []
@@ -460,7 +470,7 @@
     following = centre + spread * noise_ref[...]
     offset = following - centre
     next_ref[...] = following
-    offset_ref[...] = offset
+    density_ref[0] = jnp.mean(-offset * offset / (2.0 * spread * spread)) - level
     slope = step_size * drift_velocity * offset / (spread * spread * offset.size)
     upstream = sample_weight * slope
     grads = [
@@ -491,13 +501,13 @@
         middle_kernel,
         out_shape=(
             jax.ShapeDtypeStruct(latent.shape, jnp.float32),
-            jax.ShapeDtypeStruct(latent.shape, jnp.float32),
+            jax.ShapeDtypeStruct((1,), jnp.float32),
             jax.ShapeDtypeStruct(
                 (model_width, attended.shape[1] + final_rows.shape[1]), jnp.bfloat16
             ),
         ),
         in_specs=[pl.BlockSpec(memory_space=pltpu.SMEM)] + [whole] * 7,
-        out_specs=(whole,) * 3,
+        out_specs=(whole, pl.BlockSpec(memory_space=pltpu.SMEM), whole),
         scratch_shapes=[
             pltpu.VMEM((passes, tokens, model_width), jnp.float32),
             pltpu.VMEM((passes * tokens, model_width), jnp.bfloat16),
@@ -519,17 +529,17 @@
     modulated = (normed * (1.0 + mod_values[:, 1:2]) + mod_values[:, 0:1]).astype(jnp.bfloat16)
     stacked = modulated.reshape(2 * row_count, model_width)
     dp_size, line_size = lax.axis_size("dp"), lax.axis_size("fsdp")
-    blocks = jnp.concatenate([jnp.swapaxes(w_qkv, 0, 1), w_out[None]], 0)
+    blocks = jnp.swapaxes(w_qkv, 0, 1)
     patch = w_final.shape[1]
     group_column = jnp.broadcast_to(
         group_id[:, None].astype(jnp.bfloat16), (w_final.shape[0], patch)
     )
     thin = jnp.concatenate([w_final, group_column], 1)
-    gathered, all_thin = gather_rows(blocks, thin, dp_size, line_size)
-    gathered = gathered.reshape(4, model_width, head_columns)
+    gathered, out_rows, all_thin = gather_rows(blocks, w_out, thin, dp_size, line_size)
+    gathered = gathered.reshape(3, model_width, head_columns)
     groups = all_thin[:, 0, patch].astype(jnp.int32)
     final_rows = all_thin.reshape(model_width, -1)[:, :patch]
-    out_rows = gathered[3]
+    out_rows = out_rows.reshape(model_width, head_columns)
     attended_flat = attend(stacked, gathered, text_kv[0])
     total = head_sum(attended_flat, out_rows)
     time_now, step_size, noise_scale = plan(step_index[0], STEPS)
@@ -538,21 +548,16 @@
     drift_latent = noise_scale * noise_scale / (2.0 * time_now)
     members = jnp.sum((groups == group_id[0]).astype(jnp.float32))
     sample_weight = loss_scale * advantages[0] / members
-    scalars = jnp.stack([spread, step_size, drift_velocity, drift_latent, sample_weight])
-    following, offset, parts = middle(
+    level = jnp.log(spread) + 0.5 * math.log(2.0 * math.pi)
+    scalars = jnp.stack([spread, step_size, drift_velocity, drift_latent, sample_weight, level])
+    following, log_density, parts = middle(
         scalars, hidden[0], total, mod_values, final_rows, latents[0], noise[0],
         attended_flat.reshape(2 * row_count, head_columns),
     )
-    log_density = jnp.mean(
-        -offset * offset / (2.0 * spread * spread)
-        - jnp.log(spread)
-        - 0.5 * math.log(2.0 * math.pi)
-    )
-    sums = scatter_rows(
-        parts.reshape(dp_size * line_size, -1, parts.shape[1]), dp_size, line_size
-    )
-    grad_out, grad_final = sums[:, :head_columns], sums[:, head_columns:]
-    return (following[None], log_density[None], grad_out, grad_final)
+    grad_out, grad_final = scatter_rows(
+        parts.reshape(dp_size * line_size, -1, parts.shape[1]), head_columns, dp_size, line_size
+    )
+    return (following[None], log_density, grad_out, grad_final)
 
 
 def solution(mesh):

time: 183 us -> 176 us (0.962)
  other arithmetic: 6.53 us -> 3.58 us
    slice x3 -> x0, local copies, waits for them, and re-layouts: 2.53 us -> none  [the longest x1 1.7 us: local(): out_rows = gathered[3]]
    concatenate x1 -> x0, other arithmetic: 2.28 us -> none  [local(): blocks = jnp.concatenate([jnp.swapaxes(w_qkv, 0, 1), w_out[None]], 0)]
    unnamed x21 -> x20, local copies, waits for them, and re-layouts: 6.58 us -> 7.34 us
where the time goes in v4:
time: 176 us
  Pallas kernels  160 us (91%)
  local copies, waits for them, and re-layouts  8.09 us (5%)
  between operations  3.76 us (2%)
  other arithmetic  3.58 us (2%)
    pallas_call x1, Pallas kernels, gather_rows(): pl.pallas_call(functools.partial(gather_kernel, dp_size, line_size, ROW_F...  83.7 us
    pallas_call x1, Pallas kernels, scatter_rows(): pl.pallas_call(functools.partial(scatter_kernel, dp_size, line_size), out...  40.8 us
    pallas_call x1, Pallas kernels, head_sum(): pl.pallas_call(heads_kernel, out_shape=jax.ShapeDtypeStruct((2, 2, half,...  22.2 us
    pallas_call x1, Pallas kernels, attend(): pl.pallas_call(attend_kernel, out_shape=jax.ShapeDtypeStruct((passes, tok...  9.18 us
    unnamed x20, local copies, waits for them, and re-layouts  7.34 us
    pallas_call x1, Pallas kernels, middle(): pl.pallas_call(middle_kernel, out_shape=(jax.ShapeDtypeStruct(latent.shap...  4.33 us

profile of v4, /device:TPU:0, one launch (start us, length us, event | category | flops | bytes accessed | tf_op | source)
XLA Modules:
  0.0 175.6 jit_solution(6878110357487831826)
XLA Ops:
  0.6 0.0 copy-start
  2.4 0.9 copy.22
  3.3 0.7 concatenate.3.thin_ref
  4.0 83.7 %shard_map.138 = (bf16[3,8,304,384]{3,2,1,0:T(8,128)(2,1)}, bf16[8,304,384]{2,1,0:T(8,128)(2,1)}, bf16[8,304,128]{2,1,0:T(8,128)(2,1)}) custom-call(bf16[3,304,384]{2,1,0:T(8,128)(2,1)} %bitcast.61, bf16[304,384]{1,0:T(8,128)(2,1)} %last_ref.1, bf16[304,128]{1,0:T(8,128)(2,1)} %concatenate.3.thin_ref), custom_call_target="tpu_custom_call" | custom-call | tf_op jit(solution)/shard_map/pallas_call | solution.py:251
  87.6 1.4 fusion.6
  90.3 0.1 stack.27.scalar_ref
  90.4 0.8 bitcast_convert_fusion.mods_ref
  91.2 0.0 copy-done
  91.3 0.0 copy-start.5
  91.3 0.2 convert_reduce_fusion
  91.5 0.5 fusion.1
  92.0 0.6 fusion.5.rows_ref
  92.6 0.0 copy-done.5
  92.6 0.1 copy.35
  92.8 0.0 copy-start.1
  92.8 9.2 %shard_map.139.attended_ref = bf16[2,128,384]{2,1,0:T(8,128)(2,1)S(1)} custom-call(bf16[256,2432]{1,0:T(8,128)(2,1)S(1)} %fusion.5.rows_ref, bf16[3,2432,384]{2,1,0:T(8,128)(2,1)} %bitcast.60, bf16[2,6,333,128]{3,2,1,0:T(8,128)(2,1)S(1)} %bitcast.52), custom_call_target="tpu_custom_call" | custom-call | tf_op jit(solution)/shard_map/pallas_call | solution.py:93
  101.9 0.0 copy-start.2
  102.0 0.0 copy-done.1
  102.0 22.2 %shard_map.140 = bf16[2,2,64,2432]{3,2,1,0:T(8,128)(2,1)S(1)} custom-call(bf16[2,128,384]{2,1,0:T(8,128)(2,1)S(1)} %shard_map.139.attended_ref, bf16[2432,384]{1,0:T(8,128)(2,1)S(1)} %bitcast.54), custom_call_target="tpu_custom_call" | custom-call | tf_op jit(solution)/shard_map/pallas_call | solution.py:420
  124.2 0.8 copy.25
  125.0 1.5 copy.26
  126.5 0.0 copy-done.2
  126.5 0.0 copy-start.3
  126.5 0.8 copy-done.3
  127.4 4.3 %shard_map.141 = (f32[128,64]{1,0:T(8,128)S(1)}, f32[1]{0:T(128)}, bf16[2432,448]{1,0:T(8,128)(2,1)S(1)}) custom-call(f32[6]{0:T(128)S(1)} %stack.27.scalar_ref, bf16[2,128,2432]{2,1,0:T(8,128)(2,1)S(1)} %bitcast.50, bf16[2,128,2432]{2,1,0:T(8,128)(2,1)S(1)} %bitcast.51, f32[2,5,2432]{2,1,0:T(8,128)S(1)} %bitcast_convert_fusion.mods_ref, ...), custom_call_target="tpu_custom_call" | custom-call | tf_op jit(solution)/shard_map/pallas_call | solution.py:500
  131.7 0.0 copy-start.4
  131.7 40.8 %shard_map.142 = (f32[304,384]{1,0:T(8,128)S(1)}, f32[304,64]{1,0:T(8,128)S(1)}) custom-call(bf16[8,304,448]{2,1,0:T(8,128)(2,1)S(1)} %bitcast.53), custom_call_target="tpu_custom_call" | custom-call | tf_op jit(solution)/shard_map/pallas_call | solution.py:351
  172.5 0.0 copy-done.4
  172.5 0.8 copy.28
  173.2 1.5 copy.27
  174.8 0.8 copy.40
  (4 shorter events, 0.1 us)
Async XLA Ops:
  0.6 90.6 %copy-start = (bf16[1,2,128,2432]{3,2,1,0:T(8,128)(2,1)S(1)}, bf16[1,2,128,2432]{3,2,1,0:T(8,128)(2,1)}, u32[]{:S(2)}) copy-start(bf16[1,2,128,2432]{3,2,1,0:T(8,128)(2,1)} %param.11) | copy-start | bytes 3735556
  91.3 1.4 copy-start.5
  92.8 9.2 %copy-start.1 = (bf16[8,304,384]{2,1,0:T(8,128)(2,1)S(1)}, bf16[8,304,384]{2,1,0:T(8,128)(2,1)}, u32[]{:S(2)}) copy-start(bf16[8,304,384]{2,1,0:T(8,128)(2,1)} %get-tuple-element.14) | copy-start | bytes 5603332
  101.9 24.6 %copy-start.2 = (bf16[8,304,128]{2,1,0:T(8,128)(2,1)S(1)}, bf16[8,304,128]{2,1,0:T(8,128)(2,1)}, u32[]{:S(2)}) copy-start(bf16[8,304,128]{2,1,0:T(8,128)(2,1)} %get-tuple-element.12) | copy-start | bytes 1867780
  126.5 0.8 copy-start.3
  131.7 40.8 %copy-start.4 = (f32[128,64]{1,0:T(8,128)}, f32[128,64]{1,0:T(8,128)S(1)}, u32[]{:S(2)}) copy-start(f32[128,64]{1,0:T(8,128)S(1)} %get-tuple-element.15) | copy-start | bytes 98308
